TPU v7x, 512 devices: a whole 4x8x8 slice. The times are simulated.
512 devices in a mesh: seq: 8 (over x, core), exp: 64 (over z, y).
Axes of the slice: x: 4, y: 8, z: 8, core: 2. Of those that a mesh axis runs over, the one named last changes fastest.
Arguments:
- tokens: bfloat16 [64, 2048, 1280], P('exp', 'seq'), may hold values from -14 to 14
- slot_keys: bfloat16 [1280, 256], P('seq'), may hold values from -1 to 1
- expert_in: bfloat16 [64, 1280, 5120], P('exp', None, 'seq'), may hold values from -0.3125 to 0.3125
- expert_out: bfloat16 [64, 5120, 1280], P('exp', 'seq'), may hold values from -0.15625 to 0.15625
Outputs:
- mixed: bfloat16 [64, 2048, 1280], P('exp', 'seq')
All inputs are finite; a program needn't handle non-finite values.
Results may differ from a plain program's by a relative error of at most 0.029.
Values may be sent and summed in bfloat16 or wider, within the bound.
A program may use at most 64 MiB of HBM per device.

v0:
```python
import jax
import jax.numpy as jnp
from jax import lax
from jax.sharding import PartitionSpec as P


def key_product(flat_tokens, section):
    return jnp.dot(flat_tokens, section, preferred_element_type=jnp.float32)


def expert_hidden(pre_act):
    return jax.nn.gelu(pre_act, approximate=True).astype(jnp.bfloat16)


def on_device(tokens, slot_keys, expert_in, expert_out):
    images_here, patches_here, width = tokens.shape
    window = lax.axis_size("exp")
    flat_tokens = tokens.reshape(images_here * patches_here, width)
    logits = key_product(flat_tokens, lax.all_gather(slot_keys, "seq", axis=0, tiled=True))
    combine = jax.nn.softmax(logits, axis=1)[:, :window].astype(jnp.bfloat16)
    combine = combine.reshape(images_here, patches_here, window)
    scores = logits[:, :window].reshape(images_here, patches_here, window)
    col_max = lax.pmax(jnp.max(scores, axis=1), "seq")
    raised = jnp.exp(scores - col_max[:, None, :])
    totals = lax.psum(jnp.sum(raised, axis=1), "seq")
    dispatch = (raised / totals[:, None, :]).astype(jnp.bfloat16)
    partial_value = jnp.einsum("ipk,ipd->kid", dispatch, tokens, preferred_element_type=jnp.float32)
    w_first = expert_in[0]
    w_second = expert_out[0]
    slot_inputs = lax.psum(partial_value.astype(jnp.bfloat16), "seq")
    arrived = lax.all_to_all(slot_inputs, "exp", split_axis=0, concat_axis=1, tiled=True)
    pre_act = jnp.dot(arrived[0], w_first, preferred_element_type=jnp.float32)
    hidden = expert_hidden(pre_act)
    out_part = jnp.dot(hidden, w_second, preferred_element_type=jnp.float32)[None]
    slot_outputs = lax.psum(out_part.astype(jnp.bfloat16), "seq")
    returned = lax.all_to_all(slot_outputs, "exp", split_axis=1, concat_axis=0, tiled=True)
    mixed = jnp.einsum("ipk,kid->ipd", combine, returned, preferred_element_type=jnp.float32)
    return mixed.astype(jnp.bfloat16)


def solution(mesh):
    return jax.shard_map(
        on_device,
        mesh=mesh,
        in_specs=(
            P("exp", "seq", None),
            P("seq", None),
            P("exp", None, "seq"),
            P("exp", "seq", None),
        ),
        out_specs=P("exp", "seq", None),
        check_vma=False,
    )
```

profile of v0, /device:TPU:1, one launch (start us, length us, event | category | flops | bytes accessed | tf_op | source)
XLA Modules:
  0.0 252.8 jit_solution(6366750714011089332)
XLA Ops:
  6.5 0.0 copy-start
  6.5 0.0 copy-start.1
  6.5 0.0 all-reduce.3.cloned.1.call-start
  6.5 20.3 %all_gather.3 = bf16[1280,256]{1,0:T(8,128)(2,1)S(1)} all-gather(bf16[160,256]{1,0:T(8,128)(2,1)} %param.5), channel_id=1, replica_groups=mesh['seq'=8,'exp'=64] {'seq'}, dimensions={0}, use_global_device_ids=true | all-gather | bytes 737280 | tf_op jit(solution)/shard_map/all_gather | solution.py:19
  26.8 1.5 fusion.44
  28.3 0.1 slice_reduce_fusion
  28.4 11.9 %pmax.7 = f32[64]{0:T(128)S(1)} all-reduce(f32[64]{0:T(128)S(1)} %slice_reduce_fusion), channel_id=1, replica_groups=mesh['seq'=8,'exp'=64] {'seq'}, use_global_device_ids=true, to_apply=%region_3.0 | all-reduce | flops 64 | bytes 512 | tf_op jit(solution)/shard_map/pmax | solution.py:23
  40.4 0.2 fusion.34
  40.5 12.9 %psum.21 = f32[64]{0:T(128)S(1)} all-reduce(f32[64]{0:T(128)S(1)} %fusion.34), channel_id=1, replica_groups=mesh['seq'=8,'exp'=64] {'seq'}, use_global_device_ids=true, to_apply=%region_5.0 | all-reduce | flops 64 | bytes 512 | tf_op jit(solution)/shard_map/psum | solution.py:25
  53.4 0.0 copy-done.1
  53.4 1.0 fusion.1
  54.4 0.0 all-reduce.3.cloned.1.call-update
  54.4 0.0 all-reduce.5.cloned.1.call-start
  54.5 68.1 %all-reduce.3.cloned.1.call-done = bf16[64,1,1280]{2,0,1:T(8,128)(2,1)} async-done(((bf16[64,1,1280]{2,0,1:T(8,128)(2,1)}), bf16[64,1,1280]{2,0,1:T(8,128)(2,1)}) %all-reduce.3.cloned.1.call-update) | async-done | bytes 163856 | tf_op jit(solution)/shard_map/psum | solution.py:30
  122.5 0.6 broadcast.6
  123.1 2.3 reduce.4
  125.5 1.6 reshape.44
  127.1 23.9 %all_to_all.8 = bf16[64,2,640]{2,1,0:T(2,128)(2,1)} all-to-all(bf16[64,2,640]{2,1,0:T(2,128)(2,1)} %reshape.44), channel_id=1, replica_groups=mesh['seq'=8,'exp'=64] {'exp'}, dimensions={0} | all-to-all | bytes 327680 | tf_op jit(solution)/shard_map/all_to_all | solution.py:31
  151.0 2.1 reshape.45
  153.1 0.0 copy-done
  153.1 0.0 copy-done.2
  153.1 2.4 fusion.2
  155.5 0.0 all-reduce.5.cloned.1.call-update
  155.5 61.8 %all-reduce.5.cloned.1.call-done = bf16[1,64,1280]{2,1,0:T(8,128)(2,1)} async-done(((bf16[1,64,1280]{2,1,0:T(8,128)(2,1)}), bf16[1,64,1280]{2,1,0:T(8,128)(2,1)}) %all-reduce.5.cloned.1.call-update) | async-done | bytes 163856 | tf_op jit(solution)/shard_map/psum | solution.py:35
  217.3 1.2 copy.21
  218.5 1.6 reduce.5
  220.1 0.7 reshape.46
  220.8 12.0 %all-to-all-start.1 = ((bf16[64,2,640]{2,1,0:T(2,128)(2,1)}), bf16[64,2,640]{2,1,0:T(2,128)(2,1)S(1)}, u32[]{:S(2)}, u32[]{:S(2)}) async-start(bf16[64,2,640]{2,1,0:T(2,128)(2,1)} %reshape.46), calls=%async_computation.1 | async-start | bytes 327680 | tf_op jit(solution)/shard_map/all_to_all | solution.py:36
  232.9 0.1 fusion.43
  233.0 11.7 %all-to-all-done.1 = bf16[64,2,640]{2,1,0:T(2,128)(2,1)S(1)} async-done(((bf16[64,2,640]{2,1,0:T(2,128)(2,1)}), bf16[64,2,640]{2,1,0:T(2,128)(2,1)S(1)}, u32[]{:S(2)}, u32[]{:S(2)}) %all-to-all-start.1) | async-done | bytes 163872 | tf_op jit(solution)/shard_map/all_to_all | solution.py:36
  244.7 0.1 reshape.47
  244.8 1.2 fusion
  (1 shorter events, 0.0 us)
Async XLA Ops:
  6.5 146.6 %copy-start = (bf16[1,640,1280]{2,1,0:T(8,128)(2,1)S(1)}, bf16[1,640,1280]{2,1,0:T(8,128)(2,1)}, u32[]{:S(2)}) copy-start(bf16[1,640,1280]{2,1,0:T(8,128)(2,1)} %param.7) | copy-start | bytes 4915204
  6.5 46.9 %copy-start.1 = (bf16[1,256,1280]{2,1,0:T(8,128)(2,1)S(1)}, bf16[1,256,1280]{2,1,0:T(8,128)(2,1)}, u32[]{:S(2)}) copy-start(bf16[1,256,1280]{2,1,0:T(8,128)(2,1)} %param.4) | copy-start | bytes 1966084
  6.5 116.0 %all-reduce.3.cloned.1.call-start = ((), (), s32[]{:S(2)}) async-start(), calls=%async_computation.2 | async-start | bytes 327680 | tf_op jit(solution)/shard_map/psum | solution.py:30
  54.4 98.7 %copy-start.2 = (bf16[1,1280,640]{2,1,0:T(8,128)(2,1)S(1)}, bf16[1,1280,640]{2,1,0:T(8,128)(2,1)}, u32[]{:S(2)}) copy-start(bf16[1,1280,640]{2,1,0:T(8,128)(2,1)} %param.6) | copy-start | bytes 4915204
  54.4 162.9 %all-reduce.5.cloned.1.call-start = ((), (), s32[]{:S(2)}) async-start(), calls=%async_computation.3 | async-start | bytes 327680 | tf_op jit(solution)/shard_map/psum | solution.py:35
  220.8 23.8 %all-to-all-start.1 = ((bf16[64,2,640]{2,1,0:T(2,128)(2,1)}), bf16[64,2,640]{2,1,0:T(2,128)(2,1)S(1)}, u32[]{:S(2)}, u32[]{:S(2)}) async-start(bf16[64,2,640]{2,1,0:T(2,128)(2,1)} %reshape.46), calls=%async_computation.1 | async-start | bytes 327680 | tf_op jit(solution)/shard_map/all_to_all | solution.py:36
Sparse Core Ops, SparseCore 0:
  54.5 67.9 all-reduce.2
  155.7 61.6 all-reduce.4
where the time goes:
time: 254 us; the launch traced here: 253 us
  waiting for transfers between devices  142 us (56%)
  blocking collectives  69 us (27%)
  between operations  13.4 us (5%)
  starting transfers between devices  12.1 us (5%)
  local copies, waits for them, and re-layouts  6.29 us (2%)
  matrix products  6.07 us (2%)
  other arithmetic  4.34 us (2%)
    psum x1, waiting for transfers between devices, on_device(): slot_inputs = lax.psum(partial_value.astype(jnp.bfloat16), 'seq')  68.1 us
    psum x1, waiting for transfers between devices, on_device(): slot_outputs = lax.psum(out_part.astype(jnp.bfloat16), 'seq')  61.8 us
    all_to_all x1, blocking collectives, on_device(): lax.all_to_all(slot_inputs, 'exp', split_axis=0, concat_axis=1, tiled=True)  23.9 us
    all_gather x1, blocking collectives, on_device(): lax.all_gather(slot_keys, 'seq', axis=0, tiled=True)  20.3 us
    psum x1, blocking collectives, on_device(): totals = lax.psum(jnp.sum(raised, axis=1), 'seq')  12.9 us
    all_to_all x1, starting transfers between devices, on_device(): lax.all_to_all(slot_outputs, 'exp', split_axis=1, concat_axis=0, tiled=True)  12 us
    pmax x1, blocking collectives, on_device(): col_max = lax.pmax(jnp.max(scores, axis=1), 'seq')  11.9 us
    all_to_all x1, waiting for transfers between devices, on_device(): lax.all_to_all(slot_outputs, 'exp', split_axis=1, concat_axis=0, tiled=True)  11.7 us
  transfers between devices with their start and end apart: 3, of which 3 were waited for; matrix products, arithmetic and copies ran while one was open for 0% of the time, Pallas kernels for 0%

commit v1 on v0

v1 whole, which is shorter than its diff:
```python
import jax
import jax.numpy as jnp
from jax import lax
from jax.experimental import pallas as pl
from jax.experimental.pallas import tpu as pltpu
from jax.sharding import PartitionSpec as P

MESH = pl.DeviceIdType.MESH
BF = jnp.bfloat16
F32 = jnp.float32
SEQ = 8
SIDE = 8
D = 1280
HID = 640
PATCH = 256
SLOTS = 256
WINDOW = 64
ROWS = D // SEQ
HALF = D // 2
PACK = ROWS // 2
REST = PACK + ROWS
LINE = 16
TILES = D // 128
NEAR = (4, 5, 3, 6, 2, 7, 1)


def wait_bytes(ref, sem):
    pltpu.make_async_copy(ref, ref, sem).wait()


def gelu(v):
    inner = 0.7978845608028654 * (v + 0.044715 * (v * v * v))
    return 0.5 * v * (1.0 + jnp.tanh(inner))


def kernel(
    tok_hbm, keys_hbm, w1_hbm, w2_hbm, out_hbm,
    tok, keys, w1, w2, outv,
    ka_send, ka_recv, kb_send, kb_recv, kfull,
    st_send, st_recv, p_send, p_recv, q_send, q_recv,
    stage, r_send, r2_send, x_recv, y_recv, wide, xv, comb,
    load_sem, out_sem, ysem, zsem,
    ka_s, ka_r, kb_s, kb_r, kf_s, kf_r, st_s, st_r, p_s, p_r, q_s, q_r, x_s, x_r, y_s, y_r,
):
    s = lax.axis_index("seq")
    e = lax.axis_index("exp")
    z = e // SIDE
    y = lax.rem(e, SIDE)
    mine = lax.rem(s - z + SIDE, SIDE)

    def seq_peers():
        return [lax.rem(s + d, SEQ) for d in NEAR]

    def group_of(peer):
        return lax.rem(peer - z + SIDE, SIDE)

    loads = [
        pltpu.make_async_copy(keys_hbm, keys, load_sem.at[0]),
        pltpu.make_async_copy(tok_hbm.at[0], tok, load_sem.at[1]),
        pltpu.make_async_copy(w1_hbm.at[0], w1, load_sem.at[2]),
        pltpu.make_async_copy(w2_hbm.at[0], w2, load_sem.at[3]),
    ]
    barrier = pltpu.get_barrier_semaphore()
    for d in NEAR:
        pl.semaphore_signal(barrier, inc=1, device_id=(s, z * SIDE + lax.rem(y + d, SIDE)), device_id_type=MESH)
        pl.semaphore_signal(barrier, inc=1, device_id=(s, lax.rem(z + d, SIDE) * SIDE + y), device_id_type=MESH)
        pl.semaphore_signal(barrier, inc=1, device_id=(lax.rem(s + d, SEQ), e), device_id_type=MESH)
    for load in loads:
        load.start()
    stage[...] = jnp.zeros_like(stage)

    loads[0].wait()
    kk = keys[...]
    ka = jnp.concatenate([kk[:PACK, :WINDOW], kk[PACK:, :WINDOW]], axis=1)
    ka_send[...] = ka
    ka_recv[s] = ka
    kb_send[:PACK] = jnp.concatenate([kk[:PACK, WINDOW:128], kk[PACK:, WINDOW:128]], axis=1)
    kb_send[PACK:] = kk[:, 128:]
    kb_recv[s] = kb_send[...]
    pl.semaphore_wait(barrier, 21)

    def remote(src, dst, ssem, rsem, seq, exp):
        return pltpu.make_async_remote_copy(
            src_ref=src, dst_ref=dst, send_sem=ssem, recv_sem=rsem, device_id=(seq, exp), device_id_type=MESH
        )

    for peer in seq_peers():
        remote(ka_send, ka_recv.at[s], ka_s, ka_r, peer, e).start()
    for peer in seq_peers():
        remote(kb_send, kb_recv.at[s], kb_s, kb_r, peer, e).start()
    for d in NEAR:
        pl.semaphore_signal(ysem, inc=1, device_id=(s, z * SIDE + lax.rem(y + d, SIDE)), device_id_type=MESH)
    loads[1].wait()
    wait_bytes(ka_recv.at[pl.ds(0, SEQ - 1)], ka_r)
    for src in range(SEQ):
        got = ka_recv[src]
        kfull[ROWS * src : ROWS * src + PACK, :WINDOW] = got[:, :WINDOW]
        kfull[ROWS * src + PACK : ROWS * (src + 1), :WINDOW] = got[:, WINDOW:]

    scores = jnp.dot(tok[...], kfull[:, :WINDOW], preferred_element_type=F32)
    scores_t = scores.T
    top = jnp.max(scores_t, axis=1, keepdims=True)
    raised = jnp.exp(scores_t - top)
    total = jnp.sum(raised, axis=1, keepdims=True)
    lane = lax.broadcasted_iota(jnp.int32, (WINDOW, 128), 1)
    st_send[...] = jnp.where(lane < 64, top, total)
    for peer in seq_peers():
        rows = pl.ds(pl.multiple_of(group_of(peer) * SIDE, SIDE), SIDE)
        remote(st_send.at[rows], st_recv.at[s], st_s, st_r, peer, e).start()
    st_recv[s] = st_send[pl.ds(pl.multiple_of(mine * SIDE, SIDE), SIDE)]
    part = jnp.dot(raised.astype(BF), tok[...], preferred_element_type=F32)
    part = part * (1.0 / total)

    def fold(values, ref):
        for g in range(SIDE):
            block = values[g * SIDE : (g + 1) * SIDE]
            ref[g] = jnp.concatenate([block[:, :HALF], block[:, HALF:]], axis=0).astype(BF)

    def to_owners(send, recv, ssem, rsem):
        for peer in seq_peers():
            remote(send.at[group_of(peer)], recv.at[s], ssem, rsem, peer, e).start()
        recv[s] = send[mine]

    def to_lines(low, high, ref):
        for t in range(TILES):
            half = low if t < TILES // 2 else high
            c = (t % (TILES // 2)) * 128
            stage[pl.ds(t, SIDE, stride=LINE), :] = half[:, c : c + 128]
        ref[...] = stage[: SIDE * LINE].astype(BF)

    def spread(send, recv, ssem, rsem):
        x = s // 2
        here = pl.ds(pl.multiple_of(e * LINE, LINE), LINE)

        def step(j, carry):
            off = 4 + ((j + 1) // 2) * (2 * lax.rem(j, 2) - 1)
            row = lax.rem(y + off + SIDE, SIDE)
            src = send.at[pl.ds(pl.multiple_of(row * LINE, LINE), LINE)]
            to = mine * SIDE + row
            for dx in (2, 1, 3, 0):
                for core in range(2):
                    seq = lax.rem(x + dx, 4) * 2 + core
                    if dx:
                        remote(src, recv.at[here], ssem, rsem, seq, to).start()
                    else:
                        itself = jnp.logical_and(seq == s, to == e)

                        @pl.when(jnp.logical_not(itself))
                        def _():
                            remote(src, recv.at[here], ssem, rsem, seq, to).start()

                        @pl.when(itself)
                        def _():
                            pltpu.make_async_copy(src, recv.at[here], rsem).start()

            return carry

        lax.fori_loop(0, SIDE, step, 0)

    def spread_sent(recv, ssem):
        @pl.when(mine == z)
        def _():
            wait_bytes(recv.at[pl.ds(0, 63 * LINE)], ssem)

        @pl.when(mine != z)
        def _():
            wait_bytes(recv, ssem)

    def gather_lines(recv):
        wide[: 64 * LINE] = recv[...].astype(F32)
        for t in range(TILES):
            xv[:, 128 * t : 128 * (t + 1)] = wide[pl.ds(t, 64, stride=LINE), :].astype(BF)

    fold(part, p_send)
    to_owners(p_send, p_recv, p_s, p_r)
    pl.semaphore_wait(ysem, 7)
    for d in NEAR:
        pl.semaphore_signal(zsem, inc=1, device_id=(s, lax.rem(z + d, SIDE) * SIDE + y), device_id_type=MESH)

    wait_bytes(st_recv.at[pl.ds(0, SEQ - 1)], st_r)
    tops = [st_recv[i][:, 0:1] for i in range(SEQ)]
    sums = [st_recv[i][:, 64:65] for i in range(SEQ)]
    peak = tops[0]
    for i in range(1, SEQ):
        peak = jnp.maximum(peak, tops[i])
    weights = [jnp.exp(tops[i] - peak) * sums[i] for i in range(SEQ)]
    norm = weights[0]
    for i in range(1, SEQ):
        norm = norm + weights[i]
    norm = 1.0 / norm
    wait_bytes(p_recv.at[pl.ds(0, SEQ - 1)], p_r)
    low = high = None
    for i in range(SEQ):
        got = p_recv[i].astype(F32)
        w = weights[i] * norm
        a, b = got[:SIDE] * w, got[SIDE:] * w
        low, high = (a, b) if low is None else (low + a, high + b)
    to_lines(low, high, r_send)
    pl.semaphore_wait(zsem, 7)
    spread(r_send, x_recv, x_s, x_r)

    wait_bytes(kb_recv.at[pl.ds(0, SEQ - 1)], kb_r)
    for src in range(SEQ):
        got = kb_recv[src]
        kfull[ROWS * src : ROWS * src + PACK, WINDOW:128] = got[:PACK, :WINDOW]
        kfull[ROWS * src + PACK : ROWS * (src + 1), WINDOW:128] = got[:PACK, WINDOW:]
        kfull[ROWS * src : ROWS * (src + 1), 128:] = got[PACK:]
    every = jnp.dot(tok[...], kfull[...], preferred_element_type=F32)
    up = jnp.exp(every - jnp.max(every, axis=1, keepdims=True))
    comb[...] = (up[:, :WINDOW] * (1.0 / jnp.sum(up, axis=1, keepdims=True))).astype(BF)

    loads[2].wait()
    loads[3].wait()
    wait_bytes(x_recv, x_r)
    gather_lines(x_recv)
    hidden = gelu(jnp.dot(xv[...], w1[...], preferred_element_type=F32)).astype(BF)
    fold(jnp.dot(hidden, w2[...], preferred_element_type=F32), q_send)
    to_owners(q_send, q_recv, q_s, q_r)
    wait_bytes(q_recv.at[pl.ds(0, SEQ - 1)], q_r)
    low = high = None
    for i in range(SEQ):
        got = q_recv[i].astype(F32)
        a, b = got[:SIDE], got[SIDE:]
        low, high = (a, b) if low is None else (low + a, high + b)
    to_lines(low, high, r2_send)
    spread(r2_send, y_recv, y_s, y_r)
    wait_bytes(ka_recv.at[pl.ds(0, SEQ - 1)], ka_s)
    wait_bytes(kb_recv.at[pl.ds(0, SEQ - 1)], kb_s)
    wait_bytes(st_recv.at[pl.ds(0, SEQ - 1)], st_s)
    wait_bytes(p_recv.at[pl.ds(0, SEQ - 1)], p_s)
    wait_bytes(q_recv.at[pl.ds(0, SEQ - 1)], q_s)
    spread_sent(x_recv, x_s)

    wait_bytes(y_recv, y_r)
    gather_lines(y_recv)
    outs = []
    for c in range(5):
        cols = slice(256 * c, 256 * (c + 1))
        outv[:, cols] = jnp.dot(comb[...], xv[:, cols], preferred_element_type=F32).astype(BF)
        copy = pltpu.make_async_copy(outv.at[:, cols], out_hbm.at[0, :, cols], out_sem.at[c])
        copy.start()
        outs.append(copy)
    spread_sent(y_recv, y_s)
    for copy in outs:
        copy.wait()


def on_device(tokens, slot_keys, expert_in, expert_out):
    dma = pltpu.SemaphoreType.DMA
    reg = pltpu.SemaphoreType.REGULAR
    vm = pltpu.VMEM
    scratch = [
        vm((PATCH, D), BF), vm((ROWS, SLOTS), BF), vm((D, HID), BF), vm((HID, D), BF), vm((PATCH, D), BF),
        vm((PACK, 128), BF), vm((SEQ, PACK, 128), BF), vm((REST, 128), BF), vm((SEQ, REST, 128), BF), vm((D, SLOTS), BF),
        vm((WINDOW, 128), F32), vm((SEQ, SIDE, 128), F32),
        vm((SIDE, 16, HALF), BF), vm((SEQ, 16, HALF), BF), vm((SIDE, 16, HALF), BF), vm((SEQ, 16, HALF), BF),
        vm(((SIDE + 1) * LINE, 128), F32), vm((SIDE * LINE, 128), BF), vm((SIDE * LINE, 128), BF),
        vm((64 * LINE, 128), BF), vm((64 * LINE, 128), BF), vm((65 * LINE, 128), F32), vm((64, D), BF), vm((PATCH, WINDOW), BF),
        dma((4,)), dma((5,)), reg, reg,
    ] + [dma] * 16
    anywhere = pl.BlockSpec(memory_space=pl.ANY)
    return pl.pallas_call(
        kernel,
        name="moe",
        out_shape=jax.ShapeDtypeStruct(tokens.shape, BF),
        in_specs=[anywhere] * 4,
        out_specs=anywhere,
        scratch_shapes=scratch,
        compiler_params=pltpu.CompilerParams(collective_id=0, has_side_effects=True, vmem_limit_bytes=48 * 1024 * 1024),
    )(tokens, slot_keys, expert_in, expert_out)


def solution(mesh):
    return jax.shard_map(
        on_device,
        mesh=mesh,
        in_specs=(
            P("exp", "seq", None),
            P("seq", None),
            P("exp", None, "seq"),
            P("exp", "seq", None),
        ),
        out_specs=P("exp", "seq", None),
        check_vma=False,
    )
```

time: 254 us -> 67.9 us (0.27)
  waiting for transfers between devices: 142 us -> 0 us
  blocking collectives: 69 us -> 0 us
  Pallas kernels: 0 us -> 62 us
  between operations: 13.4 us -> 0.01 us
  starting transfers between devices: 12.1 us -> 0 us
  matrix products: 6.07 us -> 0 us
  other arithmetic: 4.34 us -> 0 us
    psum x2 -> x0, waiting for transfers between devices: 130 us -> none  [the longest x1 68.1 us: on_device(): slot_inputs = lax.psum(partial_value.astype(jnp.bfloat16), 'seq')]
    pallas_call x0 -> x1, Pallas kernels: none -> 62 us  [on_device(): pl.pallas_call(kernel, name='moe', out_shape=jax.ShapeDtypeStruct(tokens....]
    all_to_all x1 -> x0, blocking collectives: 23.9 us -> none  [on_device(): lax.all_to_all(slot_inputs, 'exp', split_axis=0, concat_axis=1, tiled=True)]
    all_gather x1 -> x0, blocking collectives: 20.3 us -> none  [on_device(): lax.all_gather(slot_keys, 'seq', axis=0, tiled=True)]
    psum x1 -> x0, blocking collectives: 12.9 us -> none  [on_device(): totals = lax.psum(jnp.sum(raised, axis=1), 'seq')]
    all_to_all x1 -> x0, starting transfers between devices: 12 us -> none  [on_device(): lax.all_to_all(slot_outputs, 'exp', split_axis=1, concat_axis=0, tiled=True)]
    pmax x1 -> x0, blocking collectives: 11.9 us -> none  [on_device(): col_max = lax.pmax(jnp.max(scores, axis=1), 'seq')]
    all_to_all x1 -> x0, waiting for transfers between devices: 11.7 us -> none  [on_device(): lax.all_to_all(slot_outputs, 'exp', split_axis=1, concat_axis=0, tiled=True)]
  transfers between devices with their start and end apart: 3 -> 0, of which waited for: 3 -> 0; matrix products, arithmetic and copies ran while one was open for 0% -> 0% of each run, Pallas kernels for 0% -> 0%
where the time goes in v1:
time: 67.9 us; the launch traced here: 67.7 us
  Pallas kernels  62 us (91%)
  local copies, waits for them, and re-layouts  5.67 us (8%)
    pallas_call x1, Pallas kernels, on_device(): pl.pallas_call(kernel, name='moe', out_shape=jax.ShapeDtypeStruct(tokens....  62 us
    unnamed x9, local copies, waits for them, and re-layouts  5.67 us

profile of v1, /device:TPU:1, one launch (start us, length us, event | category | flops | bytes accessed | tf_op | source)
XLA Modules:
  0.0 67.7 jit_solution(7160233284098223761)
XLA Ops:
  0.0 0.0 copy-start
  0.0 1.4 %copy-done = bf16[1,1280,640]{2,1,0:T(8,128)(2,1)S(1)} copy-done((bf16[1,1280,640]{2,1,0:T(8,128)(2,1)S(1)}, bf16[1,1280,640]{2,1,0:T(8,128)(2,1)}, u32[]{:S(2)}) %copy-start) | copy-done | bytes 1638424
  1.4 0.0 copy-start.1
  1.4 1.4 %copy-done.1 = bf16[1,640,1280]{2,1,0:T(8,128)(2,1)S(1)} copy-done((bf16[1,640,1280]{2,1,0:T(8,128)(2,1)S(1)}, bf16[1,640,1280]{2,1,0:T(8,128)(2,1)}, u32[]{:S(2)}) %copy-start.1) | copy-done | bytes 1638424
  2.9 0.0 copy-start.2
  2.9 1.1 %copy-done.2 = bf16[1,256,1280]{2,1,0:T(8,128)(2,1)S(1)} copy-done((bf16[1,256,1280]{2,1,0:T(8,128)(2,1)S(1)}, bf16[1,256,1280]{2,1,0:T(8,128)(2,1)}, u32[]{:S(2)}) %copy-start.2) | copy-done | bytes 655384
  4.0 0.0 copy-start.3
  4.0 0.9 %copy-done.3 = bf16[160,256]{1,0:T(8,128)(2,1)S(1)} copy-done((bf16[160,256]{1,0:T(8,128)(2,1)S(1)}, bf16[160,256]{1,0:T(8,128)(2,1)}, u32[]{:S(2)}) %copy-start.3) | copy-done | bytes 81944
  4.8 62.0 %moe.1 = bf16[1,256,1280]{2,1,0:T(8,128)(2,1)S(1)} custom-call(bf16[1,256,1280]{2,1,0:T(8,128)(2,1)S(1)} %copy-done.2, bf16[160,256]{1,0:T(8,128)(2,1)S(1)} %copy-done.3, bf16[1,1280,640]{2,1,0:T(8,128)(2,1)S(1)} %copy-done, bf16[1,640,1280]{2,1,0:T(8,128)(2,1)S(1)} %copy-done.1), custom_call_target="tpu_custom_call" | custom-call | tf_op jit(solution)/shard_map/moe/pallas_call | solution.py:262
  66.8 0.8 %copy.6 = bf16[1,256,1280]{2,1,0:T(8,128)(2,1)} copy(bf16[1,256,1280]{2,1,0:T(8,128)(2,1)S(1)} %moe.1) | data formatting | bytes 1310720
Async XLA Ops:
  0.0 1.4 %copy-start = (bf16[1,1280,640]{2,1,0:T(8,128)(2,1)S(1)}, bf16[1,1280,640]{2,1,0:T(8,128)(2,1)}, u32[]{:S(2)}) copy-start(bf16[1,1280,640]{2,1,0:T(8,128)(2,1)} %w1_hbm.1) | copy-start | bytes 4915204
  1.4 1.4 %copy-start.1 = (bf16[1,640,1280]{2,1,0:T(8,128)(2,1)S(1)}, bf16[1,640,1280]{2,1,0:T(8,128)(2,1)}, u32[]{:S(2)}) copy-start(bf16[1,640,1280]{2,1,0:T(8,128)(2,1)} %w2_hbm.1) | copy-start | bytes 4915204
  2.9 1.1 %copy-start.2 = (bf16[1,256,1280]{2,1,0:T(8,128)(2,1)S(1)}, bf16[1,256,1280]{2,1,0:T(8,128)(2,1)}, u32[]{:S(2)}) copy-start(bf16[1,256,1280]{2,1,0:T(8,128)(2,1)} %tok_hbm.1) | copy-start | bytes 1966084
  4.0 0.9 %copy-start.3 = (bf16[160,256]{1,0:T(8,128)(2,1)S(1)}, bf16[160,256]{1,0:T(8,128)(2,1)}, u32[]{:S(2)}) copy-start(bf16[160,256]{1,0:T(8,128)(2,1)} %keys_hbm.1) | copy-start | bytes 245764

commit v2 on v1

v2 whole, which is shorter than its diff:
```python
import jax
import jax.numpy as jnp
from jax import lax
from jax.experimental import pallas as pl
from jax.experimental.pallas import tpu as pltpu
from jax.sharding import PartitionSpec as P

MESH = pl.DeviceIdType.MESH
BF = jnp.bfloat16
F32 = jnp.float32
SEQ = 8
SIDE = 8
D = 1280
HID = 640
PATCH = 256
SLOTS = 256
WINDOW = 64
ROWS = D // SEQ
HALF = D // 2
PACK = ROWS // 2
REST = PACK + ROWS
LINE = 16
TILES = D // 128
NEAR = (4, 5, 3, 6, 2, 7, 1)


def wait_bytes(ref, sem):
    pltpu.make_async_copy(ref, ref, sem).wait()


def gelu(v):
    inner = 0.7978845608028654 * (v + 0.044715 * (v * v * v))
    return 0.5 * v * (1.0 + jnp.tanh(inner))


def kernel(
    tok_hbm, keys_hbm, w1_hbm, w2_hbm, out,
    tok, keys, w1, w2,
    ka_send, ka_recv, kb_send, kb_recv, kfull,
    st_send, st_recv, p_send, p_recv, q_send, q_recv,
    stage, r1_send, r2_send, b1_recv, b2_recv, c1_recv, c2_recv, xv, comb,
    load_sem, ysem, zsem, wsem,
    ka_s, ka_r, kb_s, kb_r, kf_s, kf_r, st_s, st_r, p_s, p_r, q_s, q_r,
    b1_s, b1_r, b2_s, b2_r, c1_s, c1_r, c2_s, c2_r,
):
    s = lax.axis_index("seq")
    e = lax.axis_index("exp")
    x, core = s // 2, lax.rem(s, 2)
    z, y = e // SIDE, lax.rem(e, SIDE)
    mine = lax.rem(s - z + SIDE, SIDE)

    def along_y(d):
        return (s, z * SIDE + lax.rem(y + d, SIDE))

    def along_z(d):
        return (s, lax.rem(z + d, SIDE) * SIDE + y)

    def along_seq(d):
        return (lax.rem(s + d, SEQ), e)

    def signal(sem, device):
        pl.semaphore_signal(sem, inc=1, device_id=device, device_id_type=MESH)

    def remote(src, dst, ssem, rsem, device):
        return pltpu.make_async_remote_copy(
            src_ref=src, dst_ref=dst, send_sem=ssem, recv_sem=rsem, device_id=device, device_id_type=MESH
        )

    def group_of(d):
        return lax.rem(s + d - z + SIDE, SIDE)

    barrier = pltpu.get_barrier_semaphore()
    for d in NEAR:
        signal(barrier, along_seq(d))
    for d in (2, 6, 1, 7):
        signal(barrier, along_y(d))
        signal(barrier, along_z(d))
    loads = [
        pltpu.make_async_copy(keys_hbm, keys, load_sem.at[0]),
        pltpu.make_async_copy(tok_hbm.at[0], tok, load_sem.at[1]),
        pltpu.make_async_copy(w1_hbm.at[0], w1, load_sem.at[2]),
        pltpu.make_async_copy(w2_hbm.at[0], w2, load_sem.at[3]),
    ]
    for load in loads:
        load.start()
    stage[...] = jnp.zeros_like(stage)

    loads[0].wait()
    kk = keys[...]
    ka = jnp.concatenate([kk[:PACK, :WINDOW], kk[PACK:, :WINDOW]], axis=1)
    ka_send[...] = ka
    ka_recv[s] = ka
    kb_send[:PACK] = jnp.concatenate([kk[:PACK, WINDOW:128], kk[PACK:, WINDOW:128]], axis=1)
    kb_send[PACK:] = kk[:, 128:]
    kb_recv[core, x] = kb_send[...]
    pl.semaphore_wait(barrier, 15)
    for d in NEAR:
        remote(ka_send, ka_recv.at[s], ka_s, ka_r, along_seq(d)).start()
    for d in (2, 6):
        signal(ysem, along_y(d))
        signal(zsem, along_z(d))
    loads[1].wait()
    wait_bytes(ka_recv.at[pl.ds(0, SEQ - 1)], ka_r)
    for src in range(SEQ):
        got = ka_recv[src]
        kfull[ROWS * src : ROWS * src + PACK, :WINDOW] = got[:, :WINDOW]
        kfull[ROWS * src + PACK : ROWS * (src + 1), :WINDOW] = got[:, WINDOW:]

    scores = jnp.dot(tok[...], kfull[:, :WINDOW], preferred_element_type=F32)
    scores_t = scores.T
    top = jnp.max(scores_t, axis=1, keepdims=True)
    raised = jnp.exp(scores_t - top)
    total = jnp.sum(raised, axis=1, keepdims=True)
    lane = lax.broadcasted_iota(jnp.int32, (WINDOW, 128), 1)
    st_send[...] = jnp.where(lane < 64, top, total)
    for d in NEAR:
        rows = pl.ds(pl.multiple_of(group_of(d) * SIDE, SIDE), SIDE)
        remote(st_send.at[rows], st_recv.at[s], st_s, st_r, along_seq(d)).start()
    st_recv[s] = st_send[pl.ds(pl.multiple_of(mine * SIDE, SIDE), SIDE)]
    part = jnp.dot(raised.astype(BF), tok[...], preferred_element_type=F32)
    part = part * (1.0 / total)

    def fold(values, ref):
        for g in range(SIDE):
            block = values[g * SIDE : (g + 1) * SIDE]
            ref[g] = jnp.concatenate([block[:, :HALF], block[:, HALF:]], axis=0).astype(BF)

    def to_owners(send, recv, ssem, rsem):
        for d in NEAR:
            remote(send.at[group_of(d)], recv.at[s], ssem, rsem, along_seq(d)).start()
        recv[s] = send[mine]

    def exchange(low, high, send, recv, ssem, rsem):
        for t in range(TILES):
            half = low if t < TILES // 2 else high
            c = (t % (TILES // 2)) * 128
            stage[pl.ds(t, SIDE, stride=LINE), :] = half[:, c : c + 128]
        send[...] = stage[: SIDE * LINE].astype(BF)
        here = recv.at[pl.ds(pl.multiple_of(y * LINE, LINE), LINE)]
        for d in NEAR:
            row = lax.rem(y + d, SIDE)
            src = send.at[pl.ds(pl.multiple_of(row * LINE, LINE), LINE)]
            remote(src, here, ssem, rsem, (s, mine * SIDE + row)).start()
        src = send.at[pl.ds(pl.multiple_of(y * LINE, LINE), LINE)]

        @pl.when(mine != z)
        def _():
            remote(src, here, ssem, rsem, (s, mine * SIDE + y)).start()

        @pl.when(mine == z)
        def _():
            pltpu.make_async_copy(src, here, rsem).start()

    def exchanged(recv, ssem):
        @pl.when(mine != z)
        def _():
            wait_bytes(recv, ssem)

        @pl.when(mine == z)
        def _():
            wait_bytes(recv.at[pl.ds(0, 7 * LINE)], ssem)

    def share(lines, recv, ssem, rsem):
        stage[: SIDE * LINE] = lines[...].astype(F32)
        parts = [stage[pl.ds(t, SIDE, stride=LINE), :] for t in range(TILES)]
        low = jnp.concatenate(parts[: TILES // 2], axis=1)
        high = jnp.concatenate(parts[TILES // 2 :], axis=1)
        recv[s] = jnp.concatenate([low, high], axis=0).astype(BF)
        for d in NEAR:
            remote(recv.at[s], recv.at[s], ssem, rsem, along_seq(d)).start()

    def unfold(recv):
        for g in range(0, SIDE, 2):
            a = recv[lax.rem(g + z, SIDE)].astype(F32)
            b = recv[lax.rem(g + 1 + z, SIDE)].astype(F32)
            rows = slice(g * SIDE, (g + 2) * SIDE)
            xv[rows, :HALF] = jnp.concatenate([a[:SIDE], b[:SIDE]], axis=0).astype(BF)
            xv[rows, HALF:] = jnp.concatenate([a[SIDE:], b[SIDE:]], axis=0).astype(BF)

    fold(part, p_send)
    to_owners(p_send, p_recv, p_s, p_r)
    pl.semaphore_wait(ysem, 2)
    pl.semaphore_wait(zsem, 2)

    @pl.when(mine != z)
    def _():
        signal(wsem, (s, mine * SIDE + y))

    wait_bytes(st_recv.at[pl.ds(0, SEQ - 1)], st_r)
    tops = [st_recv[i][:, 0:1] for i in range(SEQ)]
    sums = [st_recv[i][:, 64:65] for i in range(SEQ)]
    peak = tops[0]
    for i in range(1, SEQ):
        peak = jnp.maximum(peak, tops[i])
    weights = [jnp.exp(tops[i] - peak) * sums[i] for i in range(SEQ)]
    norm = weights[0]
    for i in range(1, SEQ):
        norm = norm + weights[i]
    norm = 1.0 / norm

    @pl.when(mine != z)
    def _():
        pl.semaphore_wait(wsem, 1)

    wait_bytes(p_recv.at[pl.ds(0, SEQ - 1)], p_r)
    low = high = None
    for i in range(SEQ):
        got = p_recv[i].astype(F32)
        w = weights[i] * norm
        a, b = got[:SIDE] * w, got[SIDE:] * w
        low, high = (a, b) if low is None else (low + a, high + b)
    exchange(low, high, r1_send, b1_recv, b1_s, b1_r)
    for d in (4, 2, 6):
        remote(kb_send, kb_recv.at[core, x], kb_s, kb_r, along_seq(d)).start()
    wait_bytes(b1_recv, b1_r)
    share(b1_recv, c1_recv, c1_s, c1_r)
    loads[2].wait()
    loads[3].wait()
    wait_bytes(c1_recv.at[pl.ds(0, SEQ - 1)], c1_r)

    unfold(c1_recv)
    hidden = gelu(jnp.dot(xv[...], w1[...], preferred_element_type=F32)).astype(BF)
    fold(jnp.dot(hidden, w2[...], preferred_element_type=F32), q_send)
    to_owners(q_send, q_recv, q_s, q_r)
    wait_bytes(q_recv.at[pl.ds(0, SEQ - 1)], q_r)
    low = high = None
    for i in range(SEQ):
        got = q_recv[i].astype(F32)
        a, b = got[:SIDE], got[SIDE:]
        low, high = (a, b) if low is None else (low + a, high + b)
    exchange(low, high, r2_send, b2_recv, b2_s, b2_r)

    wait_bytes(kb_recv.at[0, pl.ds(0, 3)], kb_r)
    forward = remote(kb_recv.at[core], kb_recv.at[core], kf_s, kf_r, (s + 1 - 2 * core, e))
    forward.start()
    forward.wait()
    for src in range(SEQ):
        got = kb_recv[src % 2, src // 2]
        kfull[ROWS * src : ROWS * src + PACK, WINDOW:128] = got[:PACK, :WINDOW]
        kfull[ROWS * src + PACK : ROWS * (src + 1), WINDOW:128] = got[:PACK, WINDOW:]
        kfull[ROWS * src : ROWS * (src + 1), 128:] = got[PACK:]
    every = jnp.dot(tok[...], kfull[...], preferred_element_type=F32)
    up = jnp.exp(every - jnp.max(every, axis=1, keepdims=True))
    comb[...] = (up[:, :WINDOW] * (1.0 / jnp.sum(up, axis=1, keepdims=True))).astype(BF)

    wait_bytes(b2_recv, b2_r)
    share(b2_recv, c2_recv, c2_s, c2_r)
    wait_bytes(ka_recv.at[pl.ds(0, SEQ - 1)], ka_s)
    wait_bytes(kb_recv.at[0, pl.ds(0, 3)], kb_s)
    wait_bytes(st_recv.at[pl.ds(0, SEQ - 1)], st_s)
    wait_bytes(p_recv.at[pl.ds(0, SEQ - 1)], p_s)
    wait_bytes(q_recv.at[pl.ds(0, SEQ - 1)], q_s)
    exchanged(b1_recv, b1_s)
    exchanged(b2_recv, b2_s)
    wait_bytes(c1_recv.at[pl.ds(0, SEQ - 1)], c1_s)

    wait_bytes(c2_recv.at[pl.ds(0, SEQ - 1)], c2_r)
    unfold(c2_recv)
    for c in range(5):
        cols = slice(256 * c, 256 * (c + 1))
        out[0, :, cols] = jnp.dot(comb[...], xv[:, cols], preferred_element_type=F32).astype(BF)
    wait_bytes(c2_recv.at[pl.ds(0, SEQ - 1)], c2_s)


def on_device(tokens, slot_keys, expert_in, expert_out):
    dma = pltpu.SemaphoreType.DMA
    reg = pltpu.SemaphoreType.REGULAR
    vm = pltpu.VMEM
    lines, folded = (SIDE * LINE, 128), (SEQ, 16, HALF)
    scratch = [
        vm((PATCH, D), BF), vm((ROWS, SLOTS), BF), vm((D, HID), BF), vm((HID, D), BF),
        vm((PACK, 128), BF), vm((SEQ, PACK, 128), BF), vm((REST, 128), BF), vm((2, 4, REST, 128), BF), vm((D, SLOTS), BF),
        vm((WINDOW, 128), F32), vm((SEQ, SIDE, 128), F32), vm(folded, BF), vm(folded, BF), vm(folded, BF), vm(folded, BF),
        vm(((SIDE + 1) * LINE, 128), F32), vm(lines, BF), vm(lines, BF), vm(lines, BF), vm(lines, BF),
        vm(folded, BF), vm(folded, BF), vm((64, D), BF), vm((PATCH, WINDOW), BF),
        dma((4,)), reg, reg, reg,
    ] + [dma] * 20
    operands = [pltpu.with_memory_space_constraint(a, pltpu.HBM) for a in (tokens, slot_keys, expert_in, expert_out)]
    return pl.pallas_call(
        kernel,
        name="moe",
        out_shape=jax.ShapeDtypeStruct(tokens.shape, BF),
        in_specs=[pl.BlockSpec(memory_space=pl.ANY)] * 4,
        out_specs=pl.BlockSpec(memory_space=pltpu.VMEM),
        scratch_shapes=scratch,
        compiler_params=pltpu.CompilerParams(collective_id=0, has_side_effects=True, vmem_limit_bytes=48 * 1024 * 1024),
    )(*operands)


def solution(mesh):
    return jax.shard_map(
        on_device,
        mesh=mesh,
        in_specs=(
            P("exp", "seq", None),
            P("seq", None),
            P("exp", None, "seq"),
            P("exp", "seq", None),
        ),
        out_specs=P("exp", "seq", None),
        check_vma=False,
    )
```

time: 67.9 us -> 49.1 us (0.72)
  Pallas kernels: 62 us -> 48.2 us
  local copies, waits for them, and re-layouts: 5.67 us -> 0.84 us
    pallas_call x1, Pallas kernels: 62 us -> 48.2 us  [on_device(): pl.pallas_call(kernel, name='moe', out_shape=jax.ShapeDtypeStruct(tokens....]
    unnamed x9 -> x1, local copies, waits for them, and re-layouts: 5.67 us -> 0.84 us
where the time goes in v2:
time: 49.1 us; the launch traced here: 49 us
  Pallas kernels  48.2 us (98%)
  local copies, waits for them, and re-layouts  0.84 us (2%)
    pallas_call x1, Pallas kernels, on_device(): pl.pallas_call(kernel, name='moe', out_shape=jax.ShapeDtypeStruct(tokens....  48.2 us

profile of v2, /device:TPU:1, one launch (start us, length us, event | category | flops | bytes accessed | tf_op | source)
XLA Modules:
  0.0 49.0 jit_solution(2064472691399585909)
XLA Ops:
  0.0 48.2 %moe.1 = bf16[1,256,1280]{2,1,0:T(8,128)(2,1)S(1)} custom-call(bf16[1,256,1280]{2,1,0:T(8,128)(2,1)} %tok_hbm.1, bf16[160,256]{1,0:T(8,128)(2,1)} %keys_hbm.1, bf16[1,1280,640]{2,1,0:T(8,128)(2,1)} %w1_hbm.1, bf16[1,640,1280]{2,1,0:T(8,128)(2,1)} %w2_hbm.1), custom_call_target="tpu_custom_call" | custom-call | tf_op jit(solution)/shard_map/moe/pallas_call | solution.py:279
  48.2 0.8 %copy.6 = bf16[1,256,1280]{2,1,0:T(8,128)(2,1)} copy(bf16[1,256,1280]{2,1,0:T(8,128)(2,1)S(1)} %moe.1) | data formatting | bytes 1310720

commit v3 on v2

--- a/solution.py
+++ b/solution.py
@@ -34,11 +34,11 @@
 
 
 def kernel(
-    tok_hbm, keys_hbm, w1_hbm, w2_hbm, out,
+    tok_hbm, keys_hbm, w1_hbm, w2_hbm, comb, mixed_in,
     tok, keys, w1, w2,
     ka_send, ka_recv, kb_send, kb_recv, kfull,
     st_send, st_recv, p_send, p_recv, q_send, q_recv,
-    stage, r1_send, r2_send, b1_recv, b2_recv, c1_recv, c2_recv, xv, comb,
+    stage, wide, r1_send, r2_send, c1_recv, c2_recv, xv,
     load_sem, ysem, zsem, wsem,
     ka_s, ka_r, kb_s, kb_r, kf_s, kf_r, st_s, st_r, p_s, p_r, q_s, q_r,
     b1_s, b1_r, b2_s, b2_r, c1_s, c1_r, c2_s, c2_r,
@@ -130,52 +130,53 @@
             remote(send.at[group_of(d)], recv.at[s], ssem, rsem, along_seq(d)).start()
         recv[s] = send[mine]
 
+    def line(row):
+        return pl.ds(pl.multiple_of(row * LINE, LINE), LINE)
+
     def exchange(low, high, send, recv, ssem, rsem):
         for t in range(TILES):
             half = low if t < TILES // 2 else high
             c = (t % (TILES // 2)) * 128
             stage[pl.ds(t, SIDE, stride=LINE), :] = half[:, c : c + 128]
         send[...] = stage[: SIDE * LINE].astype(BF)
-        here = recv.at[pl.ds(pl.multiple_of(y * LINE, LINE), LINE)]
+        here = recv.at[line(e)]
         for d in NEAR:
             row = lax.rem(y + d, SIDE)
-            src = send.at[pl.ds(pl.multiple_of(row * LINE, LINE), LINE)]
-            remote(src, here, ssem, rsem, (s, mine * SIDE + row)).start()
-        src = send.at[pl.ds(pl.multiple_of(y * LINE, LINE), LINE)]
+            remote(send.at[line(row)], here, ssem, rsem.at[y], (s, mine * SIDE + row)).start()
 
         @pl.when(mine != z)
         def _():
-            remote(src, here, ssem, rsem, (s, mine * SIDE + y)).start()
+            remote(send.at[line(y)], here, ssem, rsem.at[y], (s, mine * SIDE + y)).start()
 
         @pl.when(mine == z)
         def _():
-            pltpu.make_async_copy(src, here, rsem).start()
-
-    def exchanged(recv, ssem):
+            pltpu.make_async_copy(send.at[line(y)], here, rsem.at[y]).start()
+
+    def exchanged(send, ssem):
         @pl.when(mine != z)
         def _():
-            wait_bytes(recv, ssem)
+            wait_bytes(send, ssem)
 
         @pl.when(mine == z)
         def _():
-            wait_bytes(recv.at[pl.ds(0, 7 * LINE)], ssem)
-
-    def share(lines, recv, ssem, rsem):
-        stage[: SIDE * LINE] = lines[...].astype(F32)
-        parts = [stage[pl.ds(t, SIDE, stride=LINE), :] for t in range(TILES)]
-        low = jnp.concatenate(parts[: TILES // 2], axis=1)
-        high = jnp.concatenate(parts[TILES // 2 :], axis=1)
-        recv[s] = jnp.concatenate([low, high], axis=0).astype(BF)
-        for d in NEAR:
-            remote(recv.at[s], recv.at[s], ssem, rsem, along_seq(d)).start()
-
-    def unfold(recv):
-        for g in range(0, SIDE, 2):
-            a = recv[lax.rem(g + z, SIDE)].astype(F32)
-            b = recv[lax.rem(g + 1 + z, SIDE)].astype(F32)
-            rows = slice(g * SIDE, (g + 2) * SIDE)
-            xv[rows, :HALF] = jnp.concatenate([a[:SIDE], b[:SIDE]], axis=0).astype(BF)
-            xv[rows, HALF:] = jnp.concatenate([a[SIDE:], b[SIDE:]], axis=0).astype(BF)
+            wait_bytes(send.at[pl.ds(0, 7 * LINE)], ssem)
+
+    def share(recv, rsem, ssem, csem):
+        def step(j, carry):
+            half = (j + 1) // 2
+            row = lax.rem(y + SIDE + jnp.where(lax.rem(j, 2) == 1, half, -half), SIDE)
+            here = recv.at[line(mine * SIDE + row)]
+            wait_bytes(here, rsem.at[row])
+            for d in NEAR:
+                remote(here, here, ssem, csem, along_seq(d)).start()
+            return carry
+
+        lax.fori_loop(0, SIDE, step, 0)
+
+    def gather_lines(recv, ref):
+        wide[: 64 * LINE] = recv[...].astype(F32)
+        for t in range(TILES):
+            ref[:, 128 * t : 128 * (t + 1)] = wide[pl.ds(t, 64, stride=LINE), :].astype(BF)
 
     fold(part, p_send)
     to_owners(p_send, p_recv, p_s, p_r)
@@ -209,16 +210,15 @@
         w = weights[i] * norm
         a, b = got[:SIDE] * w, got[SIDE:] * w
         low, high = (a, b) if low is None else (low + a, high + b)
-    exchange(low, high, r1_send, b1_recv, b1_s, b1_r)
+    exchange(low, high, r1_send, c1_recv, b1_s, b1_r)
     for d in (4, 2, 6):
         remote(kb_send, kb_recv.at[core, x], kb_s, kb_r, along_seq(d)).start()
-    wait_bytes(b1_recv, b1_r)
-    share(b1_recv, c1_recv, c1_s, c1_r)
+    share(c1_recv, b1_r, c1_s, c1_r)
     loads[2].wait()
     loads[3].wait()
-    wait_bytes(c1_recv.at[pl.ds(0, SEQ - 1)], c1_r)
-
-    unfold(c1_recv)
+    wait_bytes(c1_recv.at[pl.ds(0, 56 * LINE)], c1_r)
+
+    gather_lines(c1_recv, xv)
     hidden = gelu(jnp.dot(xv[...], w1[...], preferred_element_type=F32)).astype(BF)
     fold(jnp.dot(hidden, w2[...], preferred_element_type=F32), q_send)
     to_owners(q_send, q_recv, q_s, q_r)
@@ -228,7 +228,7 @@
         got = q_recv[i].astype(F32)
         a, b = got[:SIDE], got[SIDE:]
         low, high = (a, b) if low is None else (low + a, high + b)
-    exchange(low, high, r2_send, b2_recv, b2_s, b2_r)
+    exchange(low, high, r2_send, c2_recv, b2_s, b2_r)
 
     wait_bytes(kb_recv.at[0, pl.ds(0, 3)], kb_r)
     forward = remote(kb_recv.at[core], kb_recv.at[core], kf_s, kf_r, (s + 1 - 2 * core, e))
@@ -243,23 +243,30 @@
     up = jnp.exp(every - jnp.max(every, axis=1, keepdims=True))
     comb[...] = (up[:, :WINDOW] * (1.0 / jnp.sum(up, axis=1, keepdims=True))).astype(BF)
 
-    wait_bytes(b2_recv, b2_r)
-    share(b2_recv, c2_recv, c2_s, c2_r)
+    share(c2_recv, b2_r, c2_s, c2_r)
     wait_bytes(ka_recv.at[pl.ds(0, SEQ - 1)], ka_s)
     wait_bytes(kb_recv.at[0, pl.ds(0, 3)], kb_s)
     wait_bytes(st_recv.at[pl.ds(0, SEQ - 1)], st_s)
     wait_bytes(p_recv.at[pl.ds(0, SEQ - 1)], p_s)
     wait_bytes(q_recv.at[pl.ds(0, SEQ - 1)], q_s)
-    exchanged(b1_recv, b1_s)
-    exchanged(b2_recv, b2_s)
-    wait_bytes(c1_recv.at[pl.ds(0, SEQ - 1)], c1_s)
-
-    wait_bytes(c2_recv.at[pl.ds(0, SEQ - 1)], c2_r)
-    unfold(c2_recv)
+    exchanged(r1_send, b1_s)
+    exchanged(r2_send, b2_s)
+    wait_bytes(c1_recv.at[pl.ds(0, 56 * LINE)], c1_s)
+
+    wait_bytes(c2_recv.at[pl.ds(0, 56 * LINE)], c2_r)
+    gather_lines(c2_recv, mixed_in)
+    wait_bytes(c2_recv.at[pl.ds(0, 56 * LINE)], c2_s)
+
+
+def mix_kernel(comb, rows, out_hbm, outv, sem):
+    copies = []
     for c in range(5):
         cols = slice(256 * c, 256 * (c + 1))
-        out[0, :, cols] = jnp.dot(comb[...], xv[:, cols], preferred_element_type=F32).astype(BF)
-    wait_bytes(c2_recv.at[pl.ds(0, SEQ - 1)], c2_s)
+        outv[:, cols] = jnp.dot(comb[...], rows[:, cols], preferred_element_type=F32).astype(BF)
+        copies.append(pltpu.make_async_copy(outv.at[:, cols], out_hbm.at[0, :, cols], sem.at[c]))
+        copies[-1].start()
+    for copy in copies:
+        copy.wait()
 
 
 def on_device(tokens, slot_keys, expert_in, expert_out):
@@ -271,20 +278,31 @@
         vm((PATCH, D), BF), vm((ROWS, SLOTS), BF), vm((D, HID), BF), vm((HID, D), BF),
         vm((PACK, 128), BF), vm((SEQ, PACK, 128), BF), vm((REST, 128), BF), vm((2, 4, REST, 128), BF), vm((D, SLOTS), BF),
         vm((WINDOW, 128), F32), vm((SEQ, SIDE, 128), F32), vm(folded, BF), vm(folded, BF), vm(folded, BF), vm(folded, BF),
-        vm(((SIDE + 1) * LINE, 128), F32), vm(lines, BF), vm(lines, BF), vm(lines, BF), vm(lines, BF),
-        vm(folded, BF), vm(folded, BF), vm((64, D), BF), vm((PATCH, WINDOW), BF),
+        vm(((SIDE + 1) * LINE, 128), F32), vm((65 * LINE, 128), F32), vm(lines, BF), vm(lines, BF),
+        vm((64 * LINE, 128), BF), vm((64 * LINE, 128), BF), vm((64, D), BF),
         dma((4,)), reg, reg, reg,
-    ] + [dma] * 20
+    ] + [dma] * 13 + [dma((SIDE,)), dma, dma((SIDE,))] + [dma] * 4
     operands = [pltpu.with_memory_space_constraint(a, pltpu.HBM) for a in (tokens, slot_keys, expert_in, expert_out)]
-    return pl.pallas_call(
+    in_vmem = pl.BlockSpec(memory_space=pltpu.VMEM)
+    anywhere = pl.BlockSpec(memory_space=pl.ANY)
+    comb, rows = pl.pallas_call(
         kernel,
         name="moe",
-        out_shape=jax.ShapeDtypeStruct(tokens.shape, BF),
-        in_specs=[pl.BlockSpec(memory_space=pl.ANY)] * 4,
-        out_specs=pl.BlockSpec(memory_space=pltpu.VMEM),
+        out_shape=(jax.ShapeDtypeStruct((PATCH, WINDOW), BF), jax.ShapeDtypeStruct((64, D), BF)),
+        in_specs=[anywhere] * 4,
+        out_specs=(in_vmem, in_vmem),
         scratch_shapes=scratch,
         compiler_params=pltpu.CompilerParams(collective_id=0, has_side_effects=True, vmem_limit_bytes=48 * 1024 * 1024),
     )(*operands)
+    return pl.pallas_call(
+        mix_kernel,
+        name="mix",
+        out_shape=jax.ShapeDtypeStruct(tokens.shape, BF),
+        in_specs=[in_vmem, in_vmem],
+        out_specs=anywhere,
+        scratch_shapes=[vm((PATCH, D), BF), dma((5,))],
+        compiler_params=pltpu.CompilerParams(vmem_limit_bytes=48 * 1024 * 1024),
+    )(comb, rows)
 
 
 def solution(mesh):

time: 49.1 us -> 50 us (1.018)
  Pallas kernels: 48.2 us -> 49.9 us
  local copies, waits for them, and re-layouts: 0.84 us -> 0 us
    pallas_call x1 -> x2, Pallas kernels: 48.2 us -> 49.9 us  [the longest x1 48.9 us: on_device(): pl.pallas_call(kernel, name='moe', out_shape=(jax.ShapeDtypeStruct((PATCH...]
    unnamed x1 -> x0, local copies, waits for them, and re-layouts: 0.84 us -> none
where the time goes in v3:
time: 50 us; the launch traced here: 49.9 us
  Pallas kernels  49.9 us (100%)
    pallas_call x1, Pallas kernels, on_device(): pl.pallas_call(kernel, name='moe', out_shape=(jax.ShapeDtypeStruct((PATCH...  48.9 us
    pallas_call x1, Pallas kernels, on_device(): pl.pallas_call(mix_kernel, name='mix', out_shape=jax.ShapeDtypeStruct(tok...  1.06 us

profile of v3, /device:TPU:1, one launch (start us, length us, event | category | flops | bytes accessed | tf_op | source)
XLA Modules:
  0.0 49.9 jit_solution(16076543895166107129)
XLA Ops:
  0.0 48.9 %moe.1 = (bf16[256,64]{1,0:T(8,128)(2,1)S(1)}, bf16[64,1280]{1,0:T(8,128)(2,1)S(1)}) custom-call(bf16[1,256,1280]{2,1,0:T(8,128)(2,1)} %tok_hbm.1, bf16[160,256]{1,0:T(8,128)(2,1)} %keys_hbm.1, bf16[1,1280,640]{2,1,0:T(8,128)(2,1)} %w1_hbm.1, bf16[1,640,1280]{2,1,0:T(8,128)(2,1)} %w2_hbm.1), custom_call_target="tpu_custom_call" | custom-call | tf_op jit(solution)/shard_map/moe/pallas_call | solution.py:288
  48.9 1.1 %mix.1 = bf16[1,256,1280]{2,1,0:T(8,128)(2,1)} custom-call(bf16[256,64]{1,0:T(8,128)(2,1)S(1)} %get-tuple-element.7.comb, bf16[64,1280]{1,0:T(8,128)(2,1)S(1)} %get-tuple-element.8.rows), custom_call_target="tpu_custom_call" | custom-call | tf_op jit(solution)/shard_map/mix/pallas_call | solution.py:297

commit v4 on v3

--- a/solution.py
+++ b/solution.py
@@ -39,7 +39,7 @@
     ka_send, ka_recv, kb_send, kb_recv, kfull,
     st_send, st_recv, p_send, p_recv, q_send, q_recv,
     stage, wide, r1_send, r2_send, c1_recv, c2_recv, xv,
-    load_sem, ysem, zsem, wsem,
+    load_sem, ysem, rsem, zsem, wsem,
     ka_s, ka_r, kb_s, kb_r, kf_s, kf_r, st_s, st_r, p_s, p_r, q_s, q_r,
     b1_s, b1_r, b2_s, b2_r, c1_s, c1_r, c2_s, c2_r,
 ):
@@ -96,9 +96,13 @@
     pl.semaphore_wait(barrier, 15)
     for d in NEAR:
         remote(ka_send, ka_recv.at[s], ka_s, ka_r, along_seq(d)).start()
+    for d in (2, 6, 1, 7):
+        signal(ysem, along_y(d))
     for d in (2, 6):
-        signal(ysem, along_y(d))
         signal(zsem, along_z(d))
+    pl.semaphore_wait(ysem, 4)
+    for d in (2, 6):
+        signal(rsem, along_y(d))
     loads[1].wait()
     wait_bytes(ka_recv.at[pl.ds(0, SEQ - 1)], ka_r)
     for src in range(SEQ):
@@ -117,6 +121,13 @@
         rows = pl.ds(pl.multiple_of(group_of(d) * SIDE, SIDE), SIDE)
         remote(st_send.at[rows], st_recv.at[s], st_s, st_r, along_seq(d)).start()
     st_recv[s] = st_send[pl.ds(pl.multiple_of(mine * SIDE, SIDE), SIDE)]
+    pl.semaphore_wait(rsem, 2)
+    pl.semaphore_wait(zsem, 2)
+
+    @pl.when(mine != z)
+    def _():
+        signal(wsem, (s, mine * SIDE + y))
+
     part = jnp.dot(raised.astype(BF), tok[...], preferred_element_type=F32)
     part = part * (1.0 / total)
 
@@ -139,53 +150,50 @@
             c = (t % (TILES // 2)) * 128
             stage[pl.ds(t, SIDE, stride=LINE), :] = half[:, c : c + 128]
         send[...] = stage[: SIDE * LINE].astype(BF)
-        here = recv.at[line(e)]
+        here = recv.at[lax.rem(z, 2), line((z // 2) * SIDE + y)]
         for d in NEAR:
             row = lax.rem(y + d, SIDE)
-            remote(send.at[line(row)], here, ssem, rsem.at[y], (s, mine * SIDE + row)).start()
+            for dx in (2, 1, 3, 0):
+                to = (lax.rem(x + dx, 4) * 2 + core, mine * SIDE + row)
+                remote(send.at[line(row)], here, ssem, rsem, to).start()
+        for dx in (2, 1, 3):
+            to = (lax.rem(x + dx, 4) * 2 + core, mine * SIDE + y)
+            remote(send.at[line(y)], here, ssem, rsem, to).start()
 
         @pl.when(mine != z)
         def _():
-            remote(send.at[line(y)], here, ssem, rsem.at[y], (s, mine * SIDE + y)).start()
+            remote(send.at[line(y)], here, ssem, rsem, (s, mine * SIDE + y)).start()
 
         @pl.when(mine == z)
         def _():
-            pltpu.make_async_copy(send.at[line(y)], here, rsem.at[y]).start()
-
-    def exchanged(send, ssem):
+            pltpu.make_async_copy(send.at[line(y)], here, rsem).start()
+
+    def exchanged(recv, ssem):
         @pl.when(mine != z)
         def _():
-            wait_bytes(send, ssem)
+            wait_bytes(recv.at[0], ssem)
 
         @pl.when(mine == z)
         def _():
-            wait_bytes(send.at[pl.ds(0, 7 * LINE)], ssem)
+            wait_bytes(recv.at[0, pl.ds(0, 31 * LINE)], ssem)
 
     def share(recv, rsem, ssem, csem):
-        def step(j, carry):
-            half = (j + 1) // 2
-            row = lax.rem(y + SIDE + jnp.where(lax.rem(j, 2) == 1, half, -half), SIDE)
-            here = recv.at[line(mine * SIDE + row)]
-            wait_bytes(here, rsem.at[row])
-            for d in NEAR:
-                remote(here, here, ssem, csem, along_seq(d)).start()
-            return carry
-
-        lax.fori_loop(0, SIDE, step, 0)
-
-    def gather_lines(recv, ref):
-        wide[: 64 * LINE] = recv[...].astype(F32)
+        own = lax.rem(core + z, 2)
+        wait_bytes(recv.at[own], rsem)
+        remote(recv.at[own], recv.at[own], ssem, csem, (s + 1 - 2 * core, e)).start()
+        wide[pl.ds(pl.multiple_of(own * 32 * LINE, 32 * LINE), 32 * LINE)] = recv[own].astype(F32)
+        other = 1 - own
+        wait_bytes(recv.at[other], csem)
+        wide[pl.ds(pl.multiple_of(other * 32 * LINE, 32 * LINE), 32 * LINE)] = recv[other].astype(F32)
+
+    def gather_lines(ref):
         for t in range(TILES):
-            ref[:, 128 * t : 128 * (t + 1)] = wide[pl.ds(t, 64, stride=LINE), :].astype(BF)
+            tile = wide[pl.ds(t, 64, stride=LINE), :]
+            groups = [tile[SIDE * ((g % 2) * 4 + g // 2) :][:SIDE] for g in range(SIDE)]
+            ref[:, 128 * t : 128 * (t + 1)] = jnp.concatenate(groups, axis=0).astype(BF)
 
     fold(part, p_send)
     to_owners(p_send, p_recv, p_s, p_r)
-    pl.semaphore_wait(ysem, 2)
-    pl.semaphore_wait(zsem, 2)
-
-    @pl.when(mine != z)
-    def _():
-        signal(wsem, (s, mine * SIDE + y))
 
     wait_bytes(st_recv.at[pl.ds(0, SEQ - 1)], st_r)
     tops = [st_recv[i][:, 0:1] for i in range(SEQ)]
@@ -213,12 +221,11 @@
     exchange(low, high, r1_send, c1_recv, b1_s, b1_r)
     for d in (4, 2, 6):
         remote(kb_send, kb_recv.at[core, x], kb_s, kb_r, along_seq(d)).start()
-    share(c1_recv, b1_r, c1_s, c1_r)
     loads[2].wait()
     loads[3].wait()
-    wait_bytes(c1_recv.at[pl.ds(0, 56 * LINE)], c1_r)
-
-    gather_lines(c1_recv, xv)
+    share(c1_recv, b1_r, c1_s, c1_r)
+
+    gather_lines(xv)
     hidden = gelu(jnp.dot(xv[...], w1[...], preferred_element_type=F32)).astype(BF)
     fold(jnp.dot(hidden, w2[...], preferred_element_type=F32), q_send)
     to_owners(q_send, q_recv, q_s, q_r)
@@ -243,19 +250,17 @@
     up = jnp.exp(every - jnp.max(every, axis=1, keepdims=True))
     comb[...] = (up[:, :WINDOW] * (1.0 / jnp.sum(up, axis=1, keepdims=True))).astype(BF)
 
-    share(c2_recv, b2_r, c2_s, c2_r)
     wait_bytes(ka_recv.at[pl.ds(0, SEQ - 1)], ka_s)
     wait_bytes(kb_recv.at[0, pl.ds(0, 3)], kb_s)
     wait_bytes(st_recv.at[pl.ds(0, SEQ - 1)], st_s)
     wait_bytes(p_recv.at[pl.ds(0, SEQ - 1)], p_s)
     wait_bytes(q_recv.at[pl.ds(0, SEQ - 1)], q_s)
-    exchanged(r1_send, b1_s)
-    exchanged(r2_send, b2_s)
-    wait_bytes(c1_recv.at[pl.ds(0, 56 * LINE)], c1_s)
-
-    wait_bytes(c2_recv.at[pl.ds(0, 56 * LINE)], c2_r)
-    gather_lines(c2_recv, mixed_in)
-    wait_bytes(c2_recv.at[pl.ds(0, 56 * LINE)], c2_s)
+    exchanged(c1_recv, b1_s)
+    wait_bytes(c1_recv.at[0], c1_s)
+    share(c2_recv, b2_r, c2_s, c2_r)
+    gather_lines(mixed_in)
+    exchanged(c2_recv, b2_s)
+    wait_bytes(c2_recv.at[0], c2_s)
 
 
 def mix_kernel(comb, rows, out_hbm, outv, sem):
@@ -279,9 +284,9 @@
         vm((PACK, 128), BF), vm((SEQ, PACK, 128), BF), vm((REST, 128), BF), vm((2, 4, REST, 128), BF), vm((D, SLOTS), BF),
         vm((WINDOW, 128), F32), vm((SEQ, SIDE, 128), F32), vm(folded, BF), vm(folded, BF), vm(folded, BF), vm(folded, BF),
         vm(((SIDE + 1) * LINE, 128), F32), vm((65 * LINE, 128), F32), vm(lines, BF), vm(lines, BF),
-        vm((64 * LINE, 128), BF), vm((64 * LINE, 128), BF), vm((64, D), BF),
-        dma((4,)), reg, reg, reg,
-    ] + [dma] * 13 + [dma((SIDE,)), dma, dma((SIDE,))] + [dma] * 4
+        vm((2, 32 * LINE, 128), BF), vm((2, 32 * LINE, 128), BF), vm((64, D), BF),
+        dma((4,)), reg, reg, reg, reg,
+    ] + [dma] * 20
     operands = [pltpu.with_memory_space_constraint(a, pltpu.HBM) for a in (tokens, slot_keys, expert_in, expert_out)]
     in_vmem = pl.BlockSpec(memory_space=pltpu.VMEM)
     anywhere = pl.BlockSpec(memory_space=pl.ANY)

time: 50 us -> 50.6 us (1.012)
  no operation moved by 1% of the time
where the time goes in v4:
time: 50.6 us; the launch traced here: 50.4 us
  Pallas kernels  50.4 us (100%)
    pallas_call x1, Pallas kernels, on_device(): pl.pallas_call(kernel, name='moe', out_shape=(jax.ShapeDtypeStruct((PATCH...  49.4 us
    pallas_call x1, Pallas kernels, on_device(): pl.pallas_call(mix_kernel, name='mix', out_shape=jax.ShapeDtypeStruct(tok...  1.06 us

profile of v4, /device:TPU:1, one launch (start us, length us, event | category | flops | bytes accessed | tf_op | source)
XLA Modules:
  0.0 50.4 jit_solution(14919926133845543711)
XLA Ops:
  0.0 49.4 %moe.1 = (bf16[256,64]{1,0:T(8,128)(2,1)S(1)}, bf16[64,1280]{1,0:T(8,128)(2,1)S(1)}) custom-call(bf16[1,256,1280]{2,1,0:T(8,128)(2,1)} %tok_hbm.1, bf16[160,256]{1,0:T(8,128)(2,1)} %keys_hbm.1, bf16[1,1280,640]{2,1,0:T(8,128)(2,1)} %w1_hbm.1, bf16[1,640,1280]{2,1,0:T(8,128)(2,1)} %w2_hbm.1), custom_call_target="tpu_custom_call" | custom-call | tf_op jit(solution)/shard_map/moe/pallas_call | solution.py:293
  49.4 1.1 %mix.1 = bf16[1,256,1280]{2,1,0:T(8,128)(2,1)} custom-call(bf16[256,64]{1,0:T(8,128)(2,1)S(1)} %get-tuple-element.7.comb, bf16[64,1280]{1,0:T(8,128)(2,1)S(1)} %get-tuple-element.8.rows), custom_call_target="tpu_custom_call" | custom-call | tf_op jit(solution)/shard_map/mix/pallas_call | solution.py:302

commit v5 on v2

--- a/solution.py
+++ b/solution.py
@@ -34,11 +34,11 @@
 
 
 def kernel(
-    tok_hbm, keys_hbm, w1_hbm, w2_hbm, out,
+    tok_hbm, keys_hbm, w1_hbm, w2_hbm, comb, mixed_in,
     tok, keys, w1, w2,
     ka_send, ka_recv, kb_send, kb_recv, kfull,
     st_send, st_recv, p_send, p_recv, q_send, q_recv,
-    stage, r1_send, r2_send, b1_recv, b2_recv, c1_recv, c2_recv, xv, comb,
+    stage, r1_send, r2_send, b1_recv, b2_recv, c1_recv, c2_recv, flat, xv,
     load_sem, ysem, zsem, wsem,
     ka_s, ka_r, kb_s, kb_r, kf_s, kf_r, st_s, st_r, p_s, p_r, q_s, q_r,
     b1_s, b1_r, b2_s, b2_r, c1_s, c1_r, c2_s, c2_r,
@@ -66,22 +66,26 @@
             src_ref=src, dst_ref=dst, send_sem=ssem, recv_sem=rsem, device_id=device, device_id_type=MESH
         )
 
-    def group_of(d):
-        return lax.rem(s + d - z + SIDE, SIDE)
-
-    barrier = pltpu.get_barrier_semaphore()
-    for d in NEAR:
-        signal(barrier, along_seq(d))
-    for d in (2, 6, 1, 7):
-        signal(barrier, along_y(d))
-        signal(barrier, along_z(d))
+    def group_of(peer):
+        return lax.rem(peer - z + SIDE, SIDE)
+
+    near_first = [s + 1 - 2 * core] + [lax.rem(x + dx, 4) * 2 + c for dx in (1, 3, 2) for c in range(2)]
+    far_first = near_first[::-1]
+
     loads = [
         pltpu.make_async_copy(keys_hbm, keys, load_sem.at[0]),
         pltpu.make_async_copy(tok_hbm.at[0], tok, load_sem.at[1]),
         pltpu.make_async_copy(w1_hbm.at[0], w1, load_sem.at[2]),
         pltpu.make_async_copy(w2_hbm.at[0], w2, load_sem.at[3]),
     ]
-    for load in loads:
+    loads[0].start()
+    barrier = pltpu.get_barrier_semaphore()
+    for peer in far_first:
+        signal(barrier, (peer, e))
+    for d in (2, 6, 1, 7):
+        signal(barrier, along_y(d))
+        signal(barrier, along_z(d))
+    for load in loads[1:]:
         load.start()
     stage[...] = jnp.zeros_like(stage)
 
@@ -94,17 +98,19 @@
     kb_send[PACK:] = kk[:, 128:]
     kb_recv[core, x] = kb_send[...]
     pl.semaphore_wait(barrier, 15)
-    for d in NEAR:
-        remote(ka_send, ka_recv.at[s], ka_s, ka_r, along_seq(d)).start()
+    for peer in far_first:
+        remote(ka_send, ka_recv.at[s], ka_s, ka_r.at[s], (peer, e)).start()
     for d in (2, 6):
         signal(ysem, along_y(d))
         signal(zsem, along_z(d))
     loads[1].wait()
-    wait_bytes(ka_recv.at[pl.ds(0, SEQ - 1)], ka_r)
-    for src in range(SEQ):
+    for src in [s] + near_first:
+        if src is not s:
+            wait_bytes(ka_recv.at[src], ka_r.at[src])
         got = ka_recv[src]
-        kfull[ROWS * src : ROWS * src + PACK, :WINDOW] = got[:, :WINDOW]
-        kfull[ROWS * src + PACK : ROWS * (src + 1), :WINDOW] = got[:, WINDOW:]
+        at = pl.multiple_of(src * ROWS, 16)
+        kfull[pl.ds(at, PACK), :WINDOW] = got[:, :WINDOW]
+        kfull[pl.ds(at + PACK, PACK), :WINDOW] = got[:, WINDOW:]
 
     scores = jnp.dot(tok[...], kfull[:, :WINDOW], preferred_element_type=F32)
     scores_t = scores.T
@@ -113,9 +119,9 @@
     total = jnp.sum(raised, axis=1, keepdims=True)
     lane = lax.broadcasted_iota(jnp.int32, (WINDOW, 128), 1)
     st_send[...] = jnp.where(lane < 64, top, total)
-    for d in NEAR:
-        rows = pl.ds(pl.multiple_of(group_of(d) * SIDE, SIDE), SIDE)
-        remote(st_send.at[rows], st_recv.at[s], st_s, st_r, along_seq(d)).start()
+    for peer in far_first:
+        rows = pl.ds(pl.multiple_of(group_of(peer) * SIDE, SIDE), SIDE)
+        remote(st_send.at[rows], st_recv.at[s], st_s, st_r, (peer, e)).start()
     st_recv[s] = st_send[pl.ds(pl.multiple_of(mine * SIDE, SIDE), SIDE)]
     part = jnp.dot(raised.astype(BF), tok[...], preferred_element_type=F32)
     part = part * (1.0 / total)
@@ -126,9 +132,23 @@
             ref[g] = jnp.concatenate([block[:, :HALF], block[:, HALF:]], axis=0).astype(BF)
 
     def to_owners(send, recv, ssem, rsem):
-        for d in NEAR:
-            remote(send.at[group_of(d)], recv.at[s], ssem, rsem, along_seq(d)).start()
-        recv[s] = send[mine]
+        for peer in far_first:
+            remote(send.at[group_of(peer)], recv.at[s], ssem, rsem.at[s], (peer, e)).start()
+
+    def owners_sum(send, recv, rsem, weight):
+        low = high = None
+        for src in [s] + near_first:
+            if src is s:
+                got = send[mine].astype(F32)
+            else:
+                wait_bytes(recv.at[src], rsem.at[src])
+                got = recv[src].astype(F32)
+            a, b = got[:SIDE], got[SIDE:]
+            if weight is not None:
+                w = weight(src)
+                a, b = a * w, b * w
+            low, high = (a, b) if low is None else (low + a, high + b)
+        return low, high
 
     def exchange(low, high, send, recv, ssem, rsem):
         for t in range(TILES):
@@ -166,16 +186,18 @@
         low = jnp.concatenate(parts[: TILES // 2], axis=1)
         high = jnp.concatenate(parts[TILES // 2 :], axis=1)
         recv[s] = jnp.concatenate([low, high], axis=0).astype(BF)
-        for d in NEAR:
-            remote(recv.at[s], recv.at[s], ssem, rsem, along_seq(d)).start()
-
-    def unfold(recv):
-        for g in range(0, SIDE, 2):
-            a = recv[lax.rem(g + z, SIDE)].astype(F32)
-            b = recv[lax.rem(g + 1 + z, SIDE)].astype(F32)
-            rows = slice(g * SIDE, (g + 2) * SIDE)
-            xv[rows, :HALF] = jnp.concatenate([a[:SIDE], b[:SIDE]], axis=0).astype(BF)
-            xv[rows, HALF:] = jnp.concatenate([a[SIDE:], b[SIDE:]], axis=0).astype(BF)
+        for peer in far_first:
+            remote(recv.at[s], recv.at[s], ssem, rsem.at[s], (peer, e)).start()
+
+    def unfold(recv, rsem, ref):
+        for src in [s] + near_first:
+            if src is not s:
+                wait_bytes(recv.at[src], rsem.at[src])
+            got = recv[src].astype(F32)
+            rows = pl.ds(pl.multiple_of(group_of(src) * SIDE, SIDE), SIDE)
+            flat[rows, :HALF] = got[:SIDE]
+            flat[rows, HALF:] = got[SIDE:]
+        ref[...] = flat[...].astype(BF)
 
     fold(part, p_send)
     to_owners(p_send, p_recv, p_s, p_r)
@@ -202,13 +224,7 @@
     def _():
         pl.semaphore_wait(wsem, 1)
 
-    wait_bytes(p_recv.at[pl.ds(0, SEQ - 1)], p_r)
-    low = high = None
-    for i in range(SEQ):
-        got = p_recv[i].astype(F32)
-        w = weights[i] * norm
-        a, b = got[:SIDE] * w, got[SIDE:] * w
-        low, high = (a, b) if low is None else (low + a, high + b)
+    low, high = owners_sum(p_send, p_recv, p_r, lambda i: jnp.exp(st_recv[i][:, 0:1] - peak) * st_recv[i][:, 64:65] * norm)
     exchange(low, high, r1_send, b1_recv, b1_s, b1_r)
     for d in (4, 2, 6):
         remote(kb_send, kb_recv.at[core, x], kb_s, kb_r, along_seq(d)).start()
@@ -216,18 +232,12 @@
     share(b1_recv, c1_recv, c1_s, c1_r)
     loads[2].wait()
     loads[3].wait()
-    wait_bytes(c1_recv.at[pl.ds(0, SEQ - 1)], c1_r)
-
-    unfold(c1_recv)
+
+    unfold(c1_recv, c1_r, xv)
     hidden = gelu(jnp.dot(xv[...], w1[...], preferred_element_type=F32)).astype(BF)
     fold(jnp.dot(hidden, w2[...], preferred_element_type=F32), q_send)
     to_owners(q_send, q_recv, q_s, q_r)
-    wait_bytes(q_recv.at[pl.ds(0, SEQ - 1)], q_r)
-    low = high = None
-    for i in range(SEQ):
-        got = q_recv[i].astype(F32)
-        a, b = got[:SIDE], got[SIDE:]
-        low, high = (a, b) if low is None else (low + a, high + b)
+    low, high = owners_sum(q_send, q_recv, q_r, None)
     exchange(low, high, r2_send, b2_recv, b2_s, b2_r)
 
     wait_bytes(kb_recv.at[0, pl.ds(0, 3)], kb_r)
@@ -254,12 +264,19 @@
     exchanged(b2_recv, b2_s)
     wait_bytes(c1_recv.at[pl.ds(0, SEQ - 1)], c1_s)
 
-    wait_bytes(c2_recv.at[pl.ds(0, SEQ - 1)], c2_r)
-    unfold(c2_recv)
+    unfold(c2_recv, c2_r, mixed_in)
+    wait_bytes(c2_recv.at[pl.ds(0, SEQ - 1)], c2_s)
+
+
+def mix_kernel(comb, rows, out_hbm, outv, sem):
+    copies = []
     for c in range(5):
         cols = slice(256 * c, 256 * (c + 1))
-        out[0, :, cols] = jnp.dot(comb[...], xv[:, cols], preferred_element_type=F32).astype(BF)
-    wait_bytes(c2_recv.at[pl.ds(0, SEQ - 1)], c2_s)
+        outv[:, cols] = jnp.dot(comb[...], rows[:, cols], preferred_element_type=F32).astype(BF)
+        copies.append(pltpu.make_async_copy(outv.at[:, cols], out_hbm.at[0, :, cols], sem.at[c]))
+        copies[-1].start()
+    for copy in copies:
+        copy.wait()
 
 
 def on_device(tokens, slot_keys, expert_in, expert_out):
@@ -272,19 +289,32 @@
         vm((PACK, 128), BF), vm((SEQ, PACK, 128), BF), vm((REST, 128), BF), vm((2, 4, REST, 128), BF), vm((D, SLOTS), BF),
         vm((WINDOW, 128), F32), vm((SEQ, SIDE, 128), F32), vm(folded, BF), vm(folded, BF), vm(folded, BF), vm(folded, BF),
         vm(((SIDE + 1) * LINE, 128), F32), vm(lines, BF), vm(lines, BF), vm(lines, BF), vm(lines, BF),
-        vm(folded, BF), vm(folded, BF), vm((64, D), BF), vm((PATCH, WINDOW), BF),
+        vm(folded, BF), vm(folded, BF), vm((64, D), F32), vm((64, D), BF),
         dma((4,)), reg, reg, reg,
-    ] + [dma] * 20
+        dma, dma((SEQ,)), dma, dma, dma, dma, dma, dma, dma, dma((SEQ,)), dma, dma((SEQ,)),
+        dma, dma, dma, dma, dma, dma((SEQ,)), dma, dma((SEQ,)),
+    ]
     operands = [pltpu.with_memory_space_constraint(a, pltpu.HBM) for a in (tokens, slot_keys, expert_in, expert_out)]
-    return pl.pallas_call(
+    in_vmem = pl.BlockSpec(memory_space=pltpu.VMEM)
+    anywhere = pl.BlockSpec(memory_space=pl.ANY)
+    comb, rows = pl.pallas_call(
         kernel,
         name="moe",
-        out_shape=jax.ShapeDtypeStruct(tokens.shape, BF),
-        in_specs=[pl.BlockSpec(memory_space=pl.ANY)] * 4,
-        out_specs=pl.BlockSpec(memory_space=pltpu.VMEM),
+        out_shape=(jax.ShapeDtypeStruct((PATCH, WINDOW), BF), jax.ShapeDtypeStruct((64, D), BF)),
+        in_specs=[anywhere] * 4,
+        out_specs=(in_vmem, in_vmem),
         scratch_shapes=scratch,
         compiler_params=pltpu.CompilerParams(collective_id=0, has_side_effects=True, vmem_limit_bytes=48 * 1024 * 1024),
     )(*operands)
+    return pl.pallas_call(
+        mix_kernel,
+        name="mix",
+        out_shape=jax.ShapeDtypeStruct(tokens.shape, BF),
+        in_specs=[in_vmem, in_vmem],
+        out_specs=anywhere,
+        scratch_shapes=[vm((PATCH, D), BF), dma((5,))],
+        compiler_params=pltpu.CompilerParams(vmem_limit_bytes=48 * 1024 * 1024),
+    )(comb, rows)
 
 
 def solution(mesh):

time: 49.1 us -> 50.2 us (1.022)
  Pallas kernels: 48.2 us -> 50.1 us
  local copies, waits for them, and re-layouts: 0.84 us -> 0 us
    pallas_call x1 -> x2, Pallas kernels: 48.2 us -> 50.1 us  [the longest x1 49 us: on_device(): pl.pallas_call(kernel, name='moe', out_shape=(jax.ShapeDtypeStruct((PATCH...]
    unnamed x1 -> x0, local copies, waits for them, and re-layouts: 0.84 us -> none
where the time goes in v5:
time: 50.2 us; the launch traced here: 50.1 us
  Pallas kernels  50.1 us (100%)
    pallas_call x1, Pallas kernels, on_device(): pl.pallas_call(kernel, name='moe', out_shape=(jax.ShapeDtypeStruct((PATCH...  49 us
    pallas_call x1, Pallas kernels, on_device(): pl.pallas_call(mix_kernel, name='mix', out_shape=jax.ShapeDtypeStruct(tok...  1.06 us

profile of v5, /device:TPU:1, one launch (start us, length us, event | category | flops | bytes accessed | tf_op | source)
XLA Modules:
  0.0 50.1 jit_solution(18206556331014302455)
XLA Ops:
  0.0 49.0 %moe.1 = (bf16[256,64]{1,0:T(8,128)(2,1)S(1)}, bf16[64,1280]{1,0:T(8,128)(2,1)S(1)}) custom-call(bf16[1,256,1280]{2,1,0:T(8,128)(2,1)} %tok_hbm.1, bf16[160,256]{1,0:T(8,128)(2,1)} %keys_hbm.1, bf16[1,1280,640]{2,1,0:T(8,128)(2,1)} %w1_hbm.1, bf16[1,640,1280]{2,1,0:T(8,128)(2,1)} %w2_hbm.1), custom_call_target="tpu_custom_call" | custom-call | tf_op jit(solution)/shard_map/moe/pallas_call | solution.py:300
  49.0 1.1 %mix.1 = bf16[1,256,1280]{2,1,0:T(8,128)(2,1)} custom-call(bf16[256,64]{1,0:T(8,128)(2,1)S(1)} %get-tuple-element.7.comb, bf16[64,1280]{1,0:T(8,128)(2,1)S(1)} %get-tuple-element.8.rows), custom_call_target="tpu_custom_call" | custom-call | tf_op jit(solution)/shard_map/mix/pallas_call | solution.py:309

commit v6 on v4

--- a/solution.py
+++ b/solution.py
@@ -47,7 +47,8 @@
     e = lax.axis_index("exp")
     x, core = s // 2, lax.rem(s, 2)
     z, y = e // SIDE, lax.rem(e, SIDE)
-    mine = lax.rem(s - z + SIDE, SIDE)
+    skew = lax.rem(z + y, SIDE)
+    mine = lax.rem(s - skew + SIDE, SIDE)
 
     def along_y(d):
         return (s, z * SIDE + lax.rem(y + d, SIDE))
@@ -67,21 +68,22 @@
         )
 
     def group_of(d):
-        return lax.rem(s + d - z + SIDE, SIDE)
-
+        return lax.rem(s + d - skew + SIDE, SIDE)
+
+    loads = [
+        pltpu.make_async_copy(keys_hbm, keys, load_sem.at[0]),
+        pltpu.make_async_copy(tok_hbm.at[0], tok, load_sem.at[1]),
+        pltpu.make_async_copy(w1_hbm.at[0], w1, load_sem.at[2]),
+        pltpu.make_async_copy(w2_hbm.at[0], w2, load_sem.at[3]),
+    ]
+    loads[0].start()
     barrier = pltpu.get_barrier_semaphore()
     for d in NEAR:
         signal(barrier, along_seq(d))
     for d in (2, 6, 1, 7):
         signal(barrier, along_y(d))
         signal(barrier, along_z(d))
-    loads = [
-        pltpu.make_async_copy(keys_hbm, keys, load_sem.at[0]),
-        pltpu.make_async_copy(tok_hbm.at[0], tok, load_sem.at[1]),
-        pltpu.make_async_copy(w1_hbm.at[0], w1, load_sem.at[2]),
-        pltpu.make_async_copy(w2_hbm.at[0], w2, load_sem.at[3]),
-    ]
-    for load in loads:
+    for load in loads[1:]:
         load.start()
     stage[...] = jnp.zeros_like(stage)
 
@@ -112,6 +114,15 @@
 
     scores = jnp.dot(tok[...], kfull[:, :WINDOW], preferred_element_type=F32)
     scores_t = scores.T
+    place = lax.rem(lax.broadcasted_iota(jnp.int32, (SIDE, PATCH), 0), SIDE)
+    groups = []
+    for g in range(SIDE):
+        block = scores_t[g * SIDE : (g + 1) * SIDE]
+        for yk in range(1, SIDE):
+            zk = (g - yk) % SIDE
+            block = jnp.where(place == yk, scores_t[zk * SIDE : (zk + 1) * SIDE], block)
+        groups.append(block)
+    scores_t = jnp.concatenate(groups, axis=0)
     top = jnp.max(scores_t, axis=1, keepdims=True)
     raised = jnp.exp(scores_t - top)
     total = jnp.sum(raised, axis=1, keepdims=True)
@@ -123,10 +134,8 @@
     st_recv[s] = st_send[pl.ds(pl.multiple_of(mine * SIDE, SIDE), SIDE)]
     pl.semaphore_wait(rsem, 2)
     pl.semaphore_wait(zsem, 2)
-
-    @pl.when(mine != z)
-    def _():
-        signal(wsem, (s, mine * SIDE + y))
+    for d in NEAR:
+        signal(wsem, along_z(d))
 
     part = jnp.dot(raised.astype(BF), tok[...], preferred_element_type=F32)
     part = part * (1.0 / total)
@@ -150,35 +159,34 @@
             c = (t % (TILES // 2)) * 128
             stage[pl.ds(t, SIDE, stride=LINE), :] = half[:, c : c + 128]
         send[...] = stage[: SIDE * LINE].astype(BF)
-        here = recv.at[lax.rem(z, 2), line((z // 2) * SIDE + y)]
-        for d in NEAR:
+        here = recv.at[lax.rem(skew, 2), line((skew // 2) * SIDE + y)]
+        for d in NEAR + (0,):
             row = lax.rem(y + d, SIDE)
+            place = lax.rem(mine - row + SIDE, SIDE) * SIDE + row
             for dx in (2, 1, 3, 0):
-                to = (lax.rem(x + dx, 4) * 2 + core, mine * SIDE + row)
-                remote(send.at[line(row)], here, ssem, rsem, to).start()
-        for dx in (2, 1, 3):
-            to = (lax.rem(x + dx, 4) * 2 + core, mine * SIDE + y)
-            remote(send.at[line(y)], here, ssem, rsem, to).start()
-
-        @pl.when(mine != z)
+                if d or dx:
+                    to = (lax.rem(x + dx, 4) * 2 + core, place)
+                    remote(send.at[line(row)], here, ssem, rsem, to).start()
+
+        @pl.when(mine != skew)
         def _():
-            remote(send.at[line(y)], here, ssem, rsem, (s, mine * SIDE + y)).start()
-
-        @pl.when(mine == z)
+            remote(send.at[line(y)], here, ssem, rsem, (s, lax.rem(mine - y + SIDE, SIDE) * SIDE + y)).start()
+
+        @pl.when(mine == skew)
         def _():
             pltpu.make_async_copy(send.at[line(y)], here, rsem).start()
 
     def exchanged(recv, ssem):
-        @pl.when(mine != z)
+        @pl.when(mine != skew)
         def _():
             wait_bytes(recv.at[0], ssem)
 
-        @pl.when(mine == z)
+        @pl.when(mine == skew)
         def _():
             wait_bytes(recv.at[0, pl.ds(0, 31 * LINE)], ssem)
 
     def share(recv, rsem, ssem, csem):
-        own = lax.rem(core + z, 2)
+        own = lax.rem(core + skew, 2)
         wait_bytes(recv.at[own], rsem)
         remote(recv.at[own], recv.at[own], ssem, csem, (s + 1 - 2 * core, e)).start()
         wide[pl.ds(pl.multiple_of(own * 32 * LINE, 32 * LINE), 32 * LINE)] = recv[own].astype(F32)
@@ -207,10 +215,7 @@
         norm = norm + weights[i]
     norm = 1.0 / norm
 
-    @pl.when(mine != z)
-    def _():
-        pl.semaphore_wait(wsem, 1)
-
+    pl.semaphore_wait(wsem, 7)
     wait_bytes(p_recv.at[pl.ds(0, SEQ - 1)], p_r)
     low = high = None
     for i in range(SEQ):
@@ -248,7 +253,11 @@
         kfull[ROWS * src : ROWS * (src + 1), 128:] = got[PACK:]
     every = jnp.dot(tok[...], kfull[...], preferred_element_type=F32)
     up = jnp.exp(every - jnp.max(every, axis=1, keepdims=True))
-    comb[...] = (up[:, :WINDOW] * (1.0 / jnp.sum(up, axis=1, keepdims=True))).astype(BF)
+    natural = (up[:, :WINDOW] * (1.0 / jnp.sum(up, axis=1, keepdims=True))).astype(BF)
+    k = lax.broadcasted_iota(jnp.int32, (WINDOW, WINDOW), 0)
+    g = lax.broadcasted_iota(jnp.int32, (WINDOW, WINDOW), 1)
+    hit = g == lax.rem(k // SIDE + lax.rem(k, SIDE), SIDE) * SIDE + lax.rem(k, SIDE)
+    comb[...] = jnp.dot(natural, jnp.where(hit, 1.0, 0.0).astype(BF), preferred_element_type=F32).astype(BF)
 
     wait_bytes(ka_recv.at[pl.ds(0, SEQ - 1)], ka_s)
     wait_bytes(kb_recv.at[0, pl.ds(0, 3)], kb_s)

time: 50.6 us -> 49.2 us (0.972)
  Pallas kernels: 50.4 us -> 49 us
    pallas_call x1, Pallas kernels: 49.4 us -> 48 us  [on_device(): pl.pallas_call(kernel, name='moe', out_shape=(jax.ShapeDtypeStruct((PATCH...]
where the time goes in v6:
time: 49.2 us; the launch traced here: 49 us
  Pallas kernels  49 us (100%)
    pallas_call x1, Pallas kernels, on_device(): pl.pallas_call(kernel, name='moe', out_shape=(jax.ShapeDtypeStruct((PATCH...  48 us
    pallas_call x1, Pallas kernels, on_device(): pl.pallas_call(mix_kernel, name='mix', out_shape=jax.ShapeDtypeStruct(tok...  1.07 us

profile of v6, /device:TPU:1, one launch (start us, length us, event | category | flops | bytes accessed | tf_op | source)
XLA Modules:
  0.0 49.0 jit_solution(3711814981940959516)
XLA Ops:
  0.0 48.0 %moe.1 = (bf16[256,64]{1,0:T(8,128)(2,1)S(1)}, bf16[64,1280]{1,0:T(8,128)(2,1)S(1)}) custom-call(bf16[1,256,1280]{2,1,0:T(8,128)(2,1)} %tok_hbm.1, bf16[160,256]{1,0:T(8,128)(2,1)} %keys_hbm.1, bf16[1,1280,640]{2,1,0:T(8,128)(2,1)} %w1_hbm.1, bf16[1,640,1280]{2,1,0:T(8,128)(2,1)} %w2_hbm.1), custom_call_target="tpu_custom_call" | custom-call | tf_op jit(solution)/shard_map/moe/pallas_call | solution.py:302
  48.0 1.1 %mix.1 = bf16[1,256,1280]{2,1,0:T(8,128)(2,1)} custom-call(bf16[256,64]{1,0:T(8,128)(2,1)S(1)} %get-tuple-element.7.comb, bf16[64,1280]{1,0:T(8,128)(2,1)S(1)} %get-tuple-element.8.rows), custom_call_target="tpu_custom_call" | custom-call | tf_op jit(solution)/shard_map/mix/pallas_call | solution.py:311

commit v7 on v6

--- a/solution.py
+++ b/solution.py
@@ -166,15 +166,15 @@
             for dx in (2, 1, 3, 0):
                 if d or dx:
                     to = (lax.rem(x + dx, 4) * 2 + core, place)
-                    remote(send.at[line(row)], here, ssem, rsem, to).start()
+                    remote(send.at[line(row)], here, ssem, rsem.at[skew // 2], to).start()
 
         @pl.when(mine != skew)
         def _():
-            remote(send.at[line(y)], here, ssem, rsem, (s, lax.rem(mine - y + SIDE, SIDE) * SIDE + y)).start()
+            remote(send.at[line(y)], here, ssem, rsem.at[skew // 2], (s, lax.rem(mine - y + SIDE, SIDE) * SIDE + y)).start()
 
         @pl.when(mine == skew)
         def _():
-            pltpu.make_async_copy(send.at[line(y)], here, rsem).start()
+            pltpu.make_async_copy(send.at[line(y)], here, rsem.at[skew // 2]).start()
 
     def exchanged(recv, ssem):
         @pl.when(mine != skew)
@@ -187,8 +187,11 @@
 
     def share(recv, rsem, ssem, csem):
         own = lax.rem(core + skew, 2)
-        wait_bytes(recv.at[own], rsem)
-        remote(recv.at[own], recv.at[own], ssem, csem, (s + 1 - 2 * core, e)).start()
+        for dx in (0, 1, 3, 2):
+            g = lax.rem(2 * lax.rem(x + dx, 4) + core - own - skew + 16, SIDE) // 2
+            eight = recv.at[own, pl.ds(pl.multiple_of(g * SIDE * LINE, SIDE * LINE), SIDE * LINE)]
+            wait_bytes(eight, rsem.at[g])
+            remote(eight, eight, ssem, csem, (s + 1 - 2 * core, e)).start()
         wide[pl.ds(pl.multiple_of(own * 32 * LINE, 32 * LINE), 32 * LINE)] = recv[own].astype(F32)
         other = 1 - own
         wait_bytes(recv.at[other], csem)
@@ -295,7 +298,7 @@
         vm(((SIDE + 1) * LINE, 128), F32), vm((65 * LINE, 128), F32), vm(lines, BF), vm(lines, BF),
         vm((2, 32 * LINE, 128), BF), vm((2, 32 * LINE, 128), BF), vm((64, D), BF),
         dma((4,)), reg, reg, reg, reg,
-    ] + [dma] * 20
+    ] + [dma] * 13 + [dma((4,)), dma, dma((4,))] + [dma] * 4
     operands = [pltpu.with_memory_space_constraint(a, pltpu.HBM) for a in (tokens, slot_keys, expert_in, expert_out)]
     in_vmem = pl.BlockSpec(memory_space=pltpu.VMEM)
     anywhere = pl.BlockSpec(memory_space=pl.ANY)

time: 49.2 us -> 49.1 us (level)
  no operation moved by 1% of the time
where the time goes in v7:
time: 49.1 us; the launch traced here: 49 us
  Pallas kernels  48.9 us (100%)
    pallas_call x1, Pallas kernels, on_device(): pl.pallas_call(kernel, name='moe', out_shape=(jax.ShapeDtypeStruct((PATCH...  47.9 us
    pallas_call x1, Pallas kernels, on_device(): pl.pallas_call(mix_kernel, name='mix', out_shape=jax.ShapeDtypeStruct(tok...  1.07 us

profile of v7, /device:TPU:1, one launch (start us, length us, event | category | flops | bytes accessed | tf_op | source)
XLA Modules:
  0.0 49.0 jit_solution(1371967401844337570)
XLA Ops:
  0.0 47.9 %moe.1 = (bf16[256,64]{1,0:T(8,128)(2,1)S(1)}, bf16[64,1280]{1,0:T(8,128)(2,1)S(1)}) custom-call(bf16[1,256,1280]{2,1,0:T(8,128)(2,1)} %tok_hbm.1, bf16[160,256]{1,0:T(8,128)(2,1)} %keys_hbm.1, bf16[1,1280,640]{2,1,0:T(8,128)(2,1)} %w1_hbm.1, bf16[1,640,1280]{2,1,0:T(8,128)(2,1)} %w2_hbm.1), custom_call_target="tpu_custom_call" | custom-call | tf_op jit(solution)/shard_map/moe/pallas_call | solution.py:305
  47.9 1.1 %mix.1 = bf16[1,256,1280]{2,1,0:T(8,128)(2,1)} custom-call(bf16[256,64]{1,0:T(8,128)(2,1)S(1)} %get-tuple-element.7.comb, bf16[64,1280]{1,0:T(8,128)(2,1)S(1)} %get-tuple-element.8.rows), custom_call_target="tpu_custom_call" | custom-call | tf_op jit(solution)/shard_map/mix/pallas_call | solution.py:314
